TPU v7x, 32 devices: a whole 2x2x4 slice. The times are simulated.
32 devices in a mesh: cluster: 8 (over z, y), feat: 4 (over x, core).
Axes of the slice: x: 2, y: 2, z: 4, core: 2. Of those that a mesh axis runs over, the one named last changes fastest.
Arguments:
- queries: bfloat16 [2048, 1024], P('cluster', 'feat'), may hold values from -6 to 6
- assign: int32 [2048, 1], P('cluster'), may hold values from 0 to 7, as said below
- band_mask: int32 [8, 7], replicated, may hold values from 0 to 1, as said below
- keys: bfloat16 [4096, 1024], P(('cluster', 'feat')), may hold values from -6 to 6
- labels: bfloat16 [4096, 1000], P(('cluster', 'feat')), may hold values from -24 to 24
- prior: bfloat16 [4096], P(('cluster', 'feat')), may hold values from -2 to 506
Outputs:
- propagated: bfloat16 [2048, 1000], P('cluster', 'feat')
Inputs may be any that keep to these rules, and one draw needn't show every extreme that they name: `assign`: in each aligned block of 256 rows at most 64 rows name one cluster. `band_mask`: entry 3 of every row is 1.
All inputs are finite; a program needn't handle non-finite values.
Results may differ from a plain program's by a relative error of at most 0.014.
Values may be sent and summed in bfloat16 or wider, within the bound.
A program may use at most 64 MiB of HBM per device.

v0:
```python
import math

import jax
import jax.numpy as jnp
from jax import lax
from jax.sharding import PartitionSpec as P

REACH = 3


temper = 2.0


def from_behind(array, axis, by):
    peers = lax.axis_size(axis)
    return lax.ppermute(array, axis, [(i, (i + by) % peers) for i in range(peers)])


def combined_all(part, axis, combine):
    gathered = jax.tree.map(lambda a: lax.all_gather(a, axis), part)

    def take(source):
        return jax.tree.map(lambda a: lax.dynamic_index_in_dim(a, source, 0, False), gathered)

    return lax.fori_loop(
        1, lax.axis_size(axis), lambda source, state: combine(state, take(source)), take(0)
    )


def combine_totals(first, second):
    top_first, sum_first = first
    top_second, sum_second = second
    highest = jnp.maximum(top_first, top_second)
    return (
        highest,
        sum_first * jnp.exp(top_first - highest) + sum_second * jnp.exp(top_second - highest),
    )


def absorb(state, block, query_full, enabled):
    running, total, accum = state
    block_keys, block_labels, block_prior = block
    scale = temper / math.sqrt(query_full.shape[1])
    scores = (
        jnp.einsum("qd,kd->qk", query_full, block_keys, preferred_element_type=jnp.float32) * scale
    )
    scores = scores + block_prior.astype(jnp.float32)[None, :]
    scores = jnp.where(enabled, scores, jnp.float32(-1e30))
    highest = jnp.maximum(running, jnp.max(scores, axis=1))
    carried = jnp.exp(running - highest)
    weight = jnp.exp(scores - highest[:, None])
    total = total * carried + jnp.sum(weight, axis=1)
    accum = accum * carried[:, None] + jnp.dot(
        weight.astype(jnp.bfloat16), block_labels, preferred_element_type=jnp.float32
    )
    return (highest, total, accum)


def body(queries, assign, band_mask, keys, labels, prior):
    clusters = lax.axis_size("cluster")
    cluster_index = lax.axis_index("cluster")
    local_rows = queries.shape[0]
    capacity = 2 * local_rows // clusters
    slots = clusters * capacity
    target = assign[:, 0]
    onehot = (target[:, None] == jnp.arange(clusters, dtype=jnp.int32)[None, :]).astype(jnp.int32)
    before = jnp.cumsum(onehot, axis=0) - onehot
    position = target * capacity + jnp.sum(before * onehot, axis=1)
    outgoing = jnp.zeros((slots, queries.shape[1]), queries.dtype).at[position].set(queries)
    arrived = lax.all_to_all(
        outgoing.reshape(clusters, capacity, queries.shape[1]),
        "cluster",
        split_axis=0,
        concat_axis=0,
        tiled=True,
    )
    query_full = lax.all_gather(
        arrived.reshape(slots, queries.shape[1]), "feat", axis=1, tiled=True
    )
    mask_row = band_mask[cluster_index]
    classes = labels.shape[1]
    state = (
        jnp.full((slots,), -1e30, jnp.float32),
        jnp.zeros((slots,), jnp.float32),
        jnp.zeros((slots, classes), jnp.float32),
    )
    state = absorb(state, (keys, labels, prior), query_full, jnp.bool_(True))

    def visit(current, block, offset):
        enabled = mask_row[REACH + offset] > 0
        return absorb(current, block, query_full, enabled)

    up_keys, up_labels, up_prior = (keys, labels, prior)
    down_keys, down_labels, down_prior = (keys, labels, prior)
    for reach in range(1, REACH + 1):
        up_keys, up_labels, up_prior = from_behind((up_keys, up_labels, up_prior), "cluster", -1)
        state = visit(state, (up_keys, up_labels, up_prior), reach)
        down_keys, down_labels, down_prior = from_behind(
            (down_keys, down_labels, down_prior), "cluster", 1
        )
        state = visit(state, (down_keys, down_labels, down_prior), -reach)
    running, total, accum = state
    highest, grand_total = combined_all((running, total), "feat", combine_totals)
    factor = jnp.exp(running - highest) / grand_total
    shares = lax.psum_scatter(
        (accum * factor[:, None]).astype(jnp.bfloat16), "feat", scatter_dimension=1, tiled=True
    )
    returned = lax.all_to_all(
        shares.reshape(clusters, capacity, shares.shape[1]),
        "cluster",
        split_axis=0,
        concat_axis=0,
        tiled=True,
    )
    return returned.reshape(slots, shares.shape[1])[position]


def solution(mesh):
    in_specs = (
        P("cluster", "feat"),
        P("cluster", None),
        P(),
        P(("cluster", "feat"), None),
        P(("cluster", "feat"), None),
        P(("cluster", "feat")),
    )
    out_specs = P("cluster", "feat")
    return jax.shard_map(body, mesh=mesh, in_specs=in_specs, out_specs=out_specs, check_vma=False)
```

profile of v0, /device:TPU:0, one launch (start us, length us, event | category | flops | bytes accessed | tf_op | source)
XLA Modules:
  0.0 196.2 jit_solution(8136210589766564269)
XLA Ops:
  8.1 0.8 fusion.53
  9.5 1.9 scatter_custom_fusion
  11.4 16.1 %all_to_all.10 = bf16[8,64,256]{2,1,0:T(8,128)(2,1)} all-to-all(bf16[8,64,256]{2,1,0:T(8,128)(2,1)S(1)} %bitcast.80), channel_id=1, replica_groups=mesh['cluster'=8,'feat'=4] {'cluster'}, dimensions={0} | all-to-all | bytes 524288 | tf_op jit(solution)/shard_map/all_to_all | solution.py:70
  27.6 2.4 %collective-permute-start = (bf16[128,1024]{1,0:T(8,128)(2,1)}, bf16[128,1024]{1,0:T(8,128)(2,1)S(1)}, u32[]{:S(2)}, u32[]{:S(2)}) collective-permute-start(bf16[128,1024]{1,0:T(8,128)(2,1)} %param.11), channel_id=1, source_target_pairs={{0,28},{4,0},{8,4},{12,8},{16,12},{20,16},{24,20},{28,24},{1,29},{... | collective-permute-start | bytes 786440 | tf_op jit(solution)/shard_map/ppermute | solution.py:16
  30.0 4.7 %collective-permute-start.2 = (bf16[128,1000]{0,1:T(8,128)(2,1)}, bf16[128,1000]{0,1:T(8,128)(2,1)S(1)}, u32[]{:S(2)}, u32[]{:S(2)}) collective-permute-start(bf16[128,1000]{0,1:T(8,128)(2,1)} %param.12), channel_id=1, source_target_pairs={{0,28},{4,0},{8,4},{12,8},{16,12},{20,16},{24,20},{28,24},{1,29},{... | collective-permute-start | bytes 768008 | tf_op jit(solution)/shard_map/ppermute | solution.py:16
  34.7 13.0 %collective-permute-done = bf16[128,1024]{1,0:T(8,128)(2,1)S(1)} collective-permute-done((bf16[128,1024]{1,0:T(8,128)(2,1)}, bf16[128,1024]{1,0:T(8,128)(2,1)S(1)}, u32[]{:S(2)}, u32[]{:S(2)}) %collective-permute-start) | collective-permute-done | bytes 262176 | tf_op jit(solution)/shard_map/ppermute | solution.py:16
  47.8 2.3 %collective-permute-start.9 = (bf16[128,1024]{1,0:T(8,128)(2,1)S(1)}, bf16[128,1024]{1,0:T(8,128)(2,1)S(1)}, u32[]{:S(2)}, u32[]{:S(2)}) collective-permute-start(bf16[128,1024]{1,0:T(8,128)(2,1)S(1)} %collective-permute-done.3), channel_id=1, source_target_pairs={{0,4},{4,8},{8,12},{12,16},{16,20},{20,24},{24,28},{28,0},{1,5},{5... | collective-permute-start | bytes 786440 | tf_op jit(solution)/shard_map/ppermute | solution.py:16
  50.1 8.6 %collective-permute-done.2 = bf16[128,1000]{0,1:T(8,128)(2,1)S(1)} collective-permute-done((bf16[128,1000]{0,1:T(8,128)(2,1)}, bf16[128,1000]{0,1:T(8,128)(2,1)S(1)}, u32[]{:S(2)}, u32[]{:S(2)}) %collective-permute-start.2) | collective-permute-done | bytes 256032 | tf_op jit(solution)/shard_map/ppermute | solution.py:16
  58.9 2.2 %collective-permute-start.11 = (bf16[128,1000]{0,1:T(8,128)(2,1)S(1)}, bf16[128,1000]{0,1:T(8,128)(2,1)}, u32[]{:S(2)}, u32[]{:S(2)}) collective-permute-start(bf16[128,1000]{0,1:T(8,128)(2,1)S(1)} %collective-permute-done.5), channel_id=1, source_target_pairs={{0,4},{4,8},{8,12},{12,16},{16,20},{20,24},{24,28},{28,0},{1,5},{5... | collective-permute-start | bytes 768008 | tf_op jit(solution)/shard_map/ppermute | solution.py:16
  61.2 2.5 %collective-permute-start.1 = (bf16[128]{0:T(256)(128)(2,1)}, bf16[128]{0:T(256)(128)(2,1)S(1)}, u32[]{:S(2)}, u32[]{:S(2)}) collective-permute-start(bf16[128]{0:T(256)(128)(2,1)} %param.13), channel_id=1, source_target_pairs={{0,28},{4,0},{8,4},{12,8},{16,12},{20,16},{24,20},{28,24},{1,29},{... | collective-permute-start | bytes 776 | tf_op jit(solution)/shard_map/ppermute | solution.py:16
  63.7 9.5 %collective-permute-done.1 = bf16[128]{0:T(256)(128)(2,1)S(1)} collective-permute-done((bf16[128]{0:T(256)(128)(2,1)}, bf16[128]{0:T(256)(128)(2,1)S(1)}, u32[]{:S(2)}, u32[]{:S(2)}) %collective-permute-start.1) | collective-permute-done | bytes 288 | tf_op jit(solution)/shard_map/ppermute | solution.py:16
  73.2 6.4 %collective-permute-done.4 = bf16[128]{0:T(256)(128)(2,1)S(1)} collective-permute-done((bf16[128]{0:T(256)(128)(2,1)}, bf16[128]{0:T(256)(128)(2,1)S(1)}, u32[]{:S(2)}, u32[]{:S(2)}) %collective-permute-start.4) | collective-permute-done | bytes 288 | tf_op jit(solution)/shard_map/ppermute | solution.py:16
  80.8 2.2 %collective-permute-done.7 = bf16[128]{0:T(256)(128)(2,1)S(1)} collective-permute-done((bf16[128]{0:T(256)(128)(2,1)S(1)}, bf16[128]{0:T(256)(128)(2,1)S(1)}, u32[]{:S(2)}, u32[]{:S(2)}) %collective-permute-start.7) | collective-permute-done | bytes 288 | tf_op jit(solution)/shard_map/ppermute | solution.py:16
  85.0 4.3 %collective-permute-done.10 = bf16[128]{0:T(256)(128)(2,1)S(1)} collective-permute-done((bf16[128]{0:T(256)(128)(2,1)S(1)}, bf16[128]{0:T(256)(128)(2,1)S(1)}, u32[]{:S(2)}, u32[]{:S(2)}) %collective-permute-start.10) | collective-permute-done | bytes 288 | tf_op jit(solution)/shard_map/ppermute | solution.py:16
  91.5 1.3 collective-permute-done.13
  93.2 6.0 %collective-permute-done.16 = bf16[128]{0:T(256)(128)(2,1)S(1)} collective-permute-done((bf16[128]{0:T(256)(128)(2,1)S(1)}, bf16[128]{0:T(256)(128)(2,1)S(1)}, u32[]{:S(2)}, u32[]{:S(2)}) %collective-permute-start.16) | collective-permute-done | bytes 288 | tf_op jit(solution)/shard_map/ppermute | solution.py:16
  99.2 1.6 collective-permute-start.14
  101.3 4.3 %collective-permute-start.12 = (bf16[128,1024]{1,0:T(8,128)(2,1)S(1)}, bf16[128,1024]{1,0:T(8,128)(2,1)S(1)}, u32[]{:S(2)}, u32[]{:S(2)}) collective-permute-start(bf16[128,1024]{1,0:T(8,128)(2,1)S(1)} %collective-permute-done.6), channel_id=1, source_target_pairs={{0,28},{4,0},{8,4},{12,8},{16,12},{20,16},{24,20},{28,24},{1,29},{... | collective-permute-start | bytes 786440 | tf_op jit(solution)/shard_map/ppermute | solution.py:16
  105.6 1.9 fusion.58
  107.5 1.7 fusion.59
  110.8 5.8 %collective-permute-done.12 = bf16[128,1024]{1,0:T(8,128)(2,1)S(1)} collective-permute-done((bf16[128,1024]{1,0:T(8,128)(2,1)S(1)}, bf16[128,1024]{1,0:T(8,128)(2,1)S(1)}, u32[]{:S(2)}, u32[]{:S(2)}) %collective-permute-start.12) | collective-permute-done | bytes 262176 | tf_op jit(solution)/shard_map/ppermute | solution.py:16
  118.2 5.2 %all-gather = f32[4,1,512]{2,1,0:T(1,128)S(1)} all-gather(f32[1,1,512]{2,1,0:T(1,128)S(1)} %get-tuple-element.167), channel_id=1, replica_groups=mesh['cluster'=8,'feat'=4] {'feat'}, dimensions={0}, use_global_device_ids=true | all-gather | bytes 10240 | tf_op jit(solution)/shard_map/all_gather | solution.py:20
  123.3 5.1 %all-gather.1 = f32[4,1,512]{2,1,0:T(1,128)S(1)} all-gather(f32[1,1,512]{2,1,0:T(1,128)S(1)} %get-tuple-element.166), channel_id=1, replica_groups=mesh['cluster'=8,'feat'=4] {'feat'}, dimensions={0}, use_global_device_ids=true | all-gather | bytes 10240 | tf_op jit(solution)/shard_map/all_gather | solution.py:20
  129.2 1.5 fusion.33
  130.7 1.5 fusion.35
  133.2 1.4 fusion.31
  134.7 3.5 %multiply_convert_fusion = bf16[512,1000]{1,0:T(8,128)(2,1)} fusion(f32[512,1000]{1,0:T(8,128)S(1)} %fusion.31, f32[512,1000]{1,0:T(8,128)S(1)} %fusion.33, f32[512,1000]{1,0:T(8,128)S(1)} %fusion.35, f32[512,1000]{1,0:T(8,128)S(1)} %fusion.37, f32[512,1000]{1,0:T(8,128)S(1)} %fusion.39, f32[512,1000]{1,0:T(8,128)S(1)} %fusion.41, ...), kind=kOutput, calls=%fused_computation.5 | convolution fusion | flops 138883072 | bytes 13848576 | tf_op jit(solution)/shard_map/dot_general | solution.py:53
  139.4 32.3 %all-reduce.3.cloned.1.call-done = bf16[512,1000]{1,0:T(8,128)(2,1)} async-done(((bf16[512,1000]{1,0:T(8,128)(2,1)}), bf16[512,1000]{1,0:T(8,128)(2,1)}) %all-reduce.3.cloned.1.call-update) | async-done | bytes 1024016
  171.7 1.9 constant_dynamic-slice_fusion.2
  173.5 5.5 %all-to-all-start.1 = ((bf16[8,64,250]{2,1,0:T(8,128)(2,1)}), bf16[8,64,250]{2,1,0:T(8,128)(2,1)S(1)}, u32[]{:S(2)}, u32[]{:S(2)}) async-start(bf16[8,64,250]{2,1,0:T(8,128)(2,1)} %bitcast.34), calls=%async_computation.1 | async-start | bytes 524288 | tf_op jit(solution)/shard_map/all_to_all | solution.py:108
  179.1 8.5 %all-to-all-done.1 = bf16[8,64,250]{2,1,0:T(8,128)(2,1)S(1)} async-done(((bf16[8,64,250]{2,1,0:T(8,128)(2,1)}), bf16[8,64,250]{2,1,0:T(8,128)(2,1)S(1)}, u32[]{:S(2)}, u32[]{:S(2)}) %all-to-all-start.1) | async-done | bytes 256032 | tf_op jit(solution)/shard_map/all_to_all | solution.py:108
  187.6 1.8 gather_fusion
  (93 shorter events, 10.5 us)
Async XLA Ops:
  6.5 66.6 %copy-start = (s32[8,7]{1,0:T(8,128)S(1)}, s32[8,7]{1,0:T(8,128)}, u32[]{:S(2)}) copy-start(s32[8,7]{1,0:T(8,128)} %param.10) | copy-start | bytes 676
  6.5 99.0 %all-gather.4.cloned.1.call-start = ((), (), s32[]{:S(2)}) async-start(), calls=%async_computation.2 | async-start | bytes 1310720 | tf_op jit(solution)/shard_map/all_gather | solution.py:77
  27.6 144.1 %all-reduce.3.cloned.1.call-start = ((), (), s32[]{:S(2)}) async-start(), calls=%async_computation.3 | async-start | bytes 2097152
  27.6 20.1 %collective-permute-start = (bf16[128,1024]{1,0:T(8,128)(2,1)}, bf16[128,1024]{1,0:T(8,128)(2,1)S(1)}, u32[]{:S(2)}, u32[]{:S(2)}) collective-permute-start(bf16[128,1024]{1,0:T(8,128)(2,1)} %param.11), channel_id=1, source_target_pairs={{0,28},{4,0},{8,4},{12,8},{16,12},{20,16},{24,20},{28,24},{1,29},{... | collective-permute-start | bytes 786440 | tf_op jit(solution)/shard_map/ppermute | solution.py:16
  30.0 17.9 %collective-permute-start.3 = (bf16[128,1024]{1,0:T(8,128)(2,1)}, bf16[128,1024]{1,0:T(8,128)(2,1)S(1)}, u32[]{:S(2)}, u32[]{:S(2)}) collective-permute-start(bf16[128,1024]{1,0:T(8,128)(2,1)} %param.11), channel_id=1, source_target_pairs={{0,4},{4,8},{8,12},{12,16},{16,20},{20,24},{24,28},{28,0},{1,5},{5... | collective-permute-start | bytes 786440 | tf_op jit(solution)/shard_map/ppermute | solution.py:16
  30.0 28.8 %collective-permute-start.2 = (bf16[128,1000]{0,1:T(8,128)(2,1)}, bf16[128,1000]{0,1:T(8,128)(2,1)S(1)}, u32[]{:S(2)}, u32[]{:S(2)}) collective-permute-start(bf16[128,1000]{0,1:T(8,128)(2,1)} %param.12), channel_id=1, source_target_pairs={{0,28},{4,0},{8,4},{12,8},{16,12},{20,16},{24,20},{28,24},{1,29},{... | collective-permute-start | bytes 768008 | tf_op jit(solution)/shard_map/ppermute | solution.py:16
  34.7 24.2 %collective-permute-start.5 = (bf16[128,1000]{0,1:T(8,128)(2,1)}, bf16[128,1000]{0,1:T(8,128)(2,1)S(1)}, u32[]{:S(2)}, u32[]{:S(2)}) collective-permute-start(bf16[128,1000]{0,1:T(8,128)(2,1)} %param.12), channel_id=1, source_target_pairs={{0,4},{4,8},{8,12},{12,16},{16,20},{20,24},{24,28},{28,0},{1,5},{5... | collective-permute-start | bytes 768008 | tf_op jit(solution)/shard_map/ppermute | solution.py:16
  47.7 53.6 %collective-permute-start.6 = (bf16[128,1024]{1,0:T(8,128)(2,1)S(1)}, bf16[128,1024]{1,0:T(8,128)(2,1)S(1)}, u32[]{:S(2)}, u32[]{:S(2)}) collective-permute-start(bf16[128,1024]{1,0:T(8,128)(2,1)S(1)} %collective-permute-done), channel_id=1, source_target_pairs={{0,28},{4,0},{8,4},{12,8},{16,12},{20,16},{24,20},{28,24},{1,29},{... | collective-permute-start | bytes 786440 | tf_op jit(solution)/shard_map/ppermute | solution.py:16
  47.8 57.7 %collective-permute-start.9 = (bf16[128,1024]{1,0:T(8,128)(2,1)S(1)}, bf16[128,1024]{1,0:T(8,128)(2,1)S(1)}, u32[]{:S(2)}, u32[]{:S(2)}) collective-permute-start(bf16[128,1024]{1,0:T(8,128)(2,1)S(1)} %collective-permute-done.3), channel_id=1, source_target_pairs={{0,4},{4,8},{8,12},{12,16},{16,20},{20,24},{24,28},{28,0},{1,5},{5... | collective-permute-start | bytes 786440 | tf_op jit(solution)/shard_map/ppermute | solution.py:16
  58.8 48.7 %copy-start.4 = (bf16[128,1000]{0,1:T(8,128)(2,1)}, bf16[128,1000]{0,1:T(8,128)(2,1)S(1)}, u32[]{:S(2)}) copy-start(bf16[128,1000]{0,1:T(8,128)(2,1)S(1)} %collective-permute-done.2) | copy-start | bytes 768004
  58.8 40.5 %collective-permute-start.8 = (bf16[128,1000]{0,1:T(8,128)(2,1)S(1)}, bf16[128,1000]{0,1:T(8,128)(2,1)}, u32[]{:S(2)}, u32[]{:S(2)}) collective-permute-start(bf16[128,1000]{0,1:T(8,128)(2,1)S(1)} %collective-permute-done.2), channel_id=1, source_target_pairs={{0,28},{4,0},{8,4},{12,8},{16,12},{20,16},{24,20},{28,24},{1,29},{... | collective-permute-start | bytes 768008 | tf_op jit(solution)/shard_map/ppermute | solution.py:16
  58.9 48.5 %copy-start.6 = (bf16[128,1000]{0,1:T(8,128)(2,1)}, bf16[128,1000]{0,1:T(8,128)(2,1)S(1)}, u32[]{:S(2)}) copy-start(bf16[128,1000]{0,1:T(8,128)(2,1)S(1)} %collective-permute-done.5) | copy-start | bytes 768004
  58.9 41.9 %collective-permute-start.11 = (bf16[128,1000]{0,1:T(8,128)(2,1)S(1)}, bf16[128,1000]{0,1:T(8,128)(2,1)}, u32[]{:S(2)}, u32[]{:S(2)}) collective-permute-start(bf16[128,1000]{0,1:T(8,128)(2,1)S(1)} %collective-permute-done.5), channel_id=1, source_target_pairs={{0,4},{4,8},{8,12},{12,16},{16,20},{20,24},{24,28},{28,0},{1,5},{5... | collective-permute-start | bytes 768008 | tf_op jit(solution)/shard_map/ppermute | solution.py:16
  61.2 12.0 %collective-permute-start.1 = (bf16[128]{0:T(256)(128)(2,1)}, bf16[128]{0:T(256)(128)(2,1)S(1)}, u32[]{:S(2)}, u32[]{:S(2)}) collective-permute-start(bf16[128]{0:T(256)(128)(2,1)} %param.13), channel_id=1, source_target_pairs={{0,28},{4,0},{8,4},{12,8},{16,12},{20,16},{24,20},{28,24},{1,29},{... | collective-permute-start | bytes 776 | tf_op jit(solution)/shard_map/ppermute | solution.py:16
  73.1 6.4 %collective-permute-start.4 = (bf16[128]{0:T(256)(128)(2,1)}, bf16[128]{0:T(256)(128)(2,1)S(1)}, u32[]{:S(2)}, u32[]{:S(2)}) collective-permute-start(bf16[128]{0:T(256)(128)(2,1)} %param.13), channel_id=1, source_target_pairs={{0,4},{4,8},{8,12},{12,16},{16,20},{20,24},{24,28},{28,0},{1,5},{5... | collective-permute-start | bytes 776 | tf_op jit(solution)/shard_map/ppermute | solution.py:16
  79.5 3.5 %collective-permute-start.7 = (bf16[128]{0:T(256)(128)(2,1)S(1)}, bf16[128]{0:T(256)(128)(2,1)S(1)}, u32[]{:S(2)}, u32[]{:S(2)}) collective-permute-start(bf16[128]{0:T(256)(128)(2,1)S(1)} %collective-permute-done.1), channel_id=1, source_target_pairs={{0,28},{4,0},{8,4},{12,8},{16,12},{20,16},{24,20},{28,24},{1,29},{... | collective-permute-start | bytes 776 | tf_op jit(solution)/shard_map/ppermute | solution.py:16
  83.1 6.2 %collective-permute-start.10 = (bf16[128]{0:T(256)(128)(2,1)S(1)}, bf16[128]{0:T(256)(128)(2,1)S(1)}, u32[]{:S(2)}, u32[]{:S(2)}) collective-permute-start(bf16[128]{0:T(256)(128)(2,1)S(1)} %collective-permute-done.4), channel_id=1, source_target_pairs={{0,4},{4,8},{8,12},{12,16},{16,20},{20,24},{24,28},{28,0},{1,5},{5... | collective-permute-start | bytes 776 | tf_op jit(solution)/shard_map/ppermute | solution.py:16
  89.3 3.5 %collective-permute-start.13 = (bf16[128]{0:T(256)(128)(2,1)S(1)}, bf16[128]{0:T(256)(128)(2,1)S(1)}, u32[]{:S(2)}, u32[]{:S(2)}) collective-permute-start(bf16[128]{0:T(256)(128)(2,1)S(1)} %collective-permute-done.7), channel_id=1, source_target_pairs={{0,28},{4,0},{8,4},{12,8},{16,12},{20,16},{24,20},{28,24},{1,29},{... | collective-permute-start | bytes 776 | tf_op jit(solution)/shard_map/ppermute | solution.py:16
  92.8 6.4 %collective-permute-start.16 = (bf16[128]{0:T(256)(128)(2,1)S(1)}, bf16[128]{0:T(256)(128)(2,1)S(1)}, u32[]{:S(2)}, u32[]{:S(2)}) collective-permute-start(bf16[128]{0:T(256)(128)(2,1)S(1)} %collective-permute-done.10), channel_id=1, source_target_pairs={{0,4},{4,8},{8,12},{12,16},{16,20},{20,24},{24,28},{28,0},{1,5},{5... | collective-permute-start | bytes 776 | tf_op jit(solution)/shard_map/ppermute | solution.py:16
  99.2 33.9 %collective-permute-start.14 = (bf16[128,1000]{0,1:T(8,128)(2,1)}, bf16[128,1000]{0,1:T(8,128)(2,1)}, u32[]{:S(2)}, u32[]{:S(2)}) collective-permute-start(bf16[128,1000]{0,1:T(8,128)(2,1)} %collective-permute-done.8), channel_id=1, source_target_pairs={{0,28},{4,0},{8,4},{12,8},{16,12},{20,16},{24,20},{28,24},{1,29},{... | collective-permute-start | bytes 768008 | tf_op jit(solution)/shard_map/ppermute | solution.py:16
  100.8 33.8 %collective-permute-start.17 = (bf16[128,1000]{0,1:T(8,128)(2,1)}, bf16[128,1000]{0,1:T(8,128)(2,1)}, u32[]{:S(2)}, u32[]{:S(2)}) collective-permute-start(bf16[128,1000]{0,1:T(8,128)(2,1)} %collective-permute-done.11), channel_id=1, source_target_pairs={{0,4},{4,8},{8,12},{12,16},{16,20},{20,24},{24,28},{28,0},{1,5},{5... | collective-permute-start | bytes 768008 | tf_op jit(solution)/shard_map/ppermute | solution.py:16
  101.3 15.3 %collective-permute-start.12 = (bf16[128,1024]{1,0:T(8,128)(2,1)S(1)}, bf16[128,1024]{1,0:T(8,128)(2,1)S(1)}, u32[]{:S(2)}, u32[]{:S(2)}) collective-permute-start(bf16[128,1024]{1,0:T(8,128)(2,1)S(1)} %collective-permute-done.6), channel_id=1, source_target_pairs={{0,28},{4,0},{8,4},{12,8},{16,12},{20,16},{24,20},{28,24},{1,29},{... | collective-permute-start | bytes 786440 | tf_op jit(solution)/shard_map/ppermute | solution.py:16
  105.6 11.6 %collective-permute-start.15 = (bf16[128,1024]{1,0:T(8,128)(2,1)S(1)}, bf16[128,1024]{1,0:T(8,128)(2,1)S(1)}, u32[]{:S(2)}, u32[]{:S(2)}) collective-permute-start(bf16[128,1024]{1,0:T(8,128)(2,1)S(1)} %collective-permute-done.9), channel_id=1, source_target_pairs={{0,4},{4,8},{8,12},{12,16},{16,20},{20,24},{24,28},{28,0},{1,5},{5... | collective-permute-start | bytes 786440 | tf_op jit(solution)/shard_map/ppermute | solution.py:16
  105.6 3.6 %copy-start.2 = (bf16[512,1024]{1,0:T(8,128)(2,1)S(1)}, bf16[512,1024]{1,0:T(8,128)(2,1)}, u32[]{:S(2)}) copy-start(bf16[512,1024]{1,0:T(8,128)(2,1)} %all-gather.4.cloned.1.call-done) | copy-start | bytes 3145732
  110.8 7.2 %copy-start.1 = (f32[512,128]{0,1:T(8,128)}, f32[512,128]{0,1:T(8,128)S(1)}, u32[]{:S(2)}) copy-start(f32[512,128]{0,1:T(8,128)S(1)} %get-tuple-element.185) | copy-start | bytes 786436
  117.1 11.4 %copy-start.3 = (bf16[128,1000]{0,1:T(8,128)(2,1)S(1)}, bf16[128,1000]{0,1:T(8,128)(2,1)}, u32[]{:S(2)}) copy-start(bf16[128,1000]{0,1:T(8,128)(2,1)} %param.12) | copy-start | bytes 768004
  129.2 3.0 %copy-start.7 = (bf16[128,1000]{0,1:T(8,128)(2,1)S(1)}, bf16[128,1000]{0,1:T(8,128)(2,1)}, u32[]{:S(2)}) copy-start(bf16[128,1000]{0,1:T(8,128)(2,1)} %copy-done.6) | copy-start | bytes 768004
  130.7 2.0 %copy-start.5 = (bf16[128,1000]{0,1:T(8,128)(2,1)S(1)}, bf16[128,1000]{0,1:T(8,128)(2,1)}, u32[]{:S(2)}) copy-start(bf16[128,1000]{0,1:T(8,128)(2,1)} %copy-done.4) | copy-start | bytes 768004
  134.6 3.5 %copy-start.8 = (u32[32]{0:T(128)S(1)}, u32[32]{0:T(128)}, u32[]{:S(2)}) copy-start(u32[32]{0:T(128)} %constant.87) | copy-start | bytes 388
  173.5 14.0 %all-to-all-start.1 = ((bf16[8,64,250]{2,1,0:T(8,128)(2,1)}), bf16[8,64,250]{2,1,0:T(8,128)(2,1)S(1)}, u32[]{:S(2)}, u32[]{:S(2)}) async-start(bf16[8,64,250]{2,1,0:T(8,128)(2,1)} %bitcast.34), calls=%async_computation.1 | async-start | bytes 524288 | tf_op jit(solution)/shard_map/all_to_all | solution.py:108
Sparse Core Ops, SparseCore 0:
  27.7 15.8 all-gather.3
  138.3 33.3 all-reduce.2
where the time goes:
time: 197 us; the launch traced here: 196 us
  waiting for transfers between devices  98.1 us (50%)
  starting transfers between devices  27.1 us (14%)
  blocking collectives  26.4 us (13%)
  between operations  18 us (9%)
  matrix products  15.4 us (8%)
  local copies, waits for them, and re-layouts  7.11 us (4%)
  other arithmetic  4.02 us (2%)
    ppermute x18, waiting for transfers between devices, from_behind(): lax.ppermute(array, axis, [(i, (i + by) % peers) for i in range(peers)])  57.3 us
    unnamed x3, waiting for transfers between devices  32.3 us
    ppermute x18, starting transfers between devices, from_behind(): lax.ppermute(array, axis, [(i, (i + by) % peers) for i in range(peers)])  21.5 us
    all_to_all x1, blocking collectives, body(): lax.all_to_all(outgoing.reshape(clusters, capacity, queries.shape[1]), 'c...  16.1 us
    all_gather x2, blocking collectives, combined_all(): gathered = jax.tree.map(lambda a: lax.all_gather(a, axis), part)  10.3 us
    dot_general x7, matrix products, absorb(): jnp.dot(weight.astype(jnp.bfloat16), block_labels, preferred_element_type...  9.33 us
    all_to_all x1, waiting for transfers between devices, body(): lax.all_to_all(shares.reshape(clusters, capacity, shares.shape[1]), 'clus...  8.52 us
    dot_general x7, matrix products, absorb(): jnp.einsum('qd,kd->qk', query_full, block_keys, preferred_element_type=jn...  6.1 us
  transfers between devices with their start and end apart: 21, of which 11 were waited for; matrix products, arithmetic and copies ran while one was open for 7% of the time, Pallas kernels for 0%

commit v1 on v0

--- a/solution.py
+++ b/solution.py
@@ -1,14 +1,300 @@
+import functools
 import math
 
 import jax
 import jax.numpy as jnp
 from jax import lax
+from jax.experimental import pallas as pl
+from jax.experimental.pallas import tpu as pltpu
 from jax.sharding import PartitionSpec as P
 
 REACH = 3
+HIDDEN = -1e30
+MESH = pl.DeviceIdType.MESH
 
 
 temper = 2.0
+
+
+def spread(row, width):
+    return jnp.broadcast_to(row, (width, row.shape[1])).T
+
+
+def widen(column, times):
+    return jnp.concatenate([column] * times, axis=1)
+
+
+def plane_kernel(
+    scale,
+    queries_ref,
+    assign_ref,
+    mask_ref,
+    keys_ref,
+    labels_ref,
+    prior_ref,
+    out_ref,
+    qbuf,
+    vbuf,
+    kbuf,
+    lbuf,
+    pbuf,
+    weights,
+    stats_own,
+    numer_own,
+    numer_out,
+    numer_in,
+    stats_in,
+    home_out,
+    home_stats_out,
+    home_in,
+    home_stats_in,
+    final_out,
+    final_in,
+    send_sem,
+    recv_sem,
+):
+    cluster = lax.axis_index("cluster")
+    feat = lax.axis_index("feat")
+    clusters = mask_ref.shape[0]
+    floors = clusters // 2
+    half = queries_ref.shape[0] // 2
+    rows = keys_ref.shape[0]
+    part = labels_ref.shape[1] // 4
+    padded = lbuf.shape[1] // 4
+    z, y = lax.div(cluster, 2), lax.rem(cluster, 2)
+    x, core = lax.div(feat, 2), lax.rem(feat, 2)
+    twin = (cluster, feat + 1 - 2 * core)
+    across = (cluster, feat + 2 - 4 * x)
+    beside = (cluster + 1 - 2 * y, feat)
+
+    def floor_peer(by):
+        return (lax.rem(cluster + 2 * by, clusters), feat)
+
+    barrier = pltpu.get_barrier_semaphore()
+    peers = [twin, across, beside] + [floor_peer(by) for by in range(1, floors)]
+    for peer in peers:
+        pl.semaphore_signal(barrier, inc=1, device_id=peer, device_id_type=MESH)
+    pl.semaphore_wait(barrier, len(peers))
+
+    started = []
+
+    def send(src, dst, peer):
+        index = len(started)
+        copy = pltpu.make_async_remote_copy(
+            src_ref=src,
+            dst_ref=dst,
+            send_sem=send_sem.at[index],
+            recv_sem=recv_sem.at[index],
+            device_id=peer,
+            device_id_type=MESH,
+        )
+        copy.start()
+        started.append(copy)
+        return copy
+
+    def block(index):
+        return pl.ds(index * rows, rows)
+
+    mine = pl.ds(pl.multiple_of(core * half, half), half)
+    other = pl.ds(pl.multiple_of((1 - core) * half, half), half)
+
+    query_twin = send(queries_ref.at[other], qbuf.at[z, x, core], twin)
+    keys_beside = send(keys_ref, kbuf.at[block(2)], beside)
+    pbuf[0] = jnp.broadcast_to(prior_ref[...].astype(jnp.float32), (8, rows))
+    prior_beside = send(pbuf.at[0], pbuf.at[2], beside)
+    keys_twin = send(keys_ref, kbuf.at[block(1)], twin)
+    prior_twin = send(pbuf.at[0], pbuf.at[1], twin)
+    qbuf[z, x, core] = queries_ref[mine, :]
+
+    assigned = assign_ref[...]
+    assigned = jnp.where(core == 0, assigned[:, :half], assigned[:, half:])
+    assigned = jnp.broadcast_to(assigned, (clusters, half))
+    row = lax.broadcasted_iota(jnp.int32, (clusters, half), 0)
+    seen = jnp.zeros((clusters, half), jnp.int32)
+    for owner in range(clusters):
+        column = jnp.zeros((clusters, half), jnp.int32)
+        for step in range(2 * REACH + 1):
+            column = jnp.where(
+                row == (owner + step - REACH) % clusters, mask_ref[owner, step], column
+            )
+        seen = jnp.where(assigned == owner, column, seen)
+    vbuf[z] = jnp.where(seen > 0, jnp.float32(0.0), jnp.float32(HIDDEN))
+    seen_floor = [None] + [send(vbuf.at[z], vbuf.at[z], floor_peer(by)) for by in range(1, floors)]
+
+    query_twin.wait_recv()
+    query_floor = [None] + [
+        send(qbuf.at[z, x], qbuf.at[z, x], floor_peer(by)) for by in range(1, floors)
+    ]
+    query_across = [send(qbuf.at[z, x], qbuf.at[z, x], across)]
+
+    lbuf[block(0), :] = jnp.zeros((rows, 4 * padded), lbuf.dtype)
+    for quarter in range(4):
+        lbuf[block(0), quarter * padded : quarter * padded + part] = labels_ref[
+            :, quarter * part : (quarter + 1) * part
+        ]
+    labels_beside = send(lbuf.at[block(0)], lbuf.at[block(2)], beside)
+    labels_twin = send(lbuf.at[block(0)], lbuf.at[block(1)], twin)
+    kbuf[block(0), :] = keys_ref[...]
+
+    def home(by):
+        return lax.rem(z - by + floors, floors)
+
+    def forward_query(by):
+        query_floor[by].wait_recv()
+        source = home(by)
+        query_across.append(send(qbuf.at[source, x], qbuf.at[source, x], across))
+
+    forward_query(1)
+    keys_beside.wait_recv()
+    prior_beside.wait_recv()
+    keys_relay = send(kbuf.at[block(2)], kbuf.at[block(3)], twin)
+    prior_relay = send(pbuf.at[2], pbuf.at[3], twin)
+    for by in range(2, floors):
+        forward_query(by)
+    for copy in (keys_twin, prior_twin, keys_relay, prior_relay):
+        copy.wait_recv()
+
+    def score(by):
+        source = home(by)
+        query_across[by].wait_recv()
+        if by > 0:
+            seen_floor[by].wait_recv()
+        width = qbuf.shape[4]
+        scores = jnp.zeros((4 * rows, half), jnp.float32)
+        for quarter in range(4):
+            scores = scores + lax.dot_general(
+                kbuf[:, quarter * width : (quarter + 1) * width],
+                qbuf[source, quarter // 2, quarter % 2],
+                (((1,), (1,)), ((), ())),
+                preferred_element_type=jnp.float32,
+            )
+        scores = scores * scale
+        near = vbuf[source, pl.ds(cluster, 1), :]
+        far = vbuf[source, pl.ds(cluster + 1 - 2 * y, 1), :]
+        pieces = []
+        for index in range(4):
+            bias = spread(pbuf[index, 0:1, :], half)
+            pieces.append(
+                scores[index * rows : (index + 1) * rows] + bias + (near if index < 2 else far)
+            )
+        scores = jnp.concatenate(pieces, axis=0)
+        top = jnp.max(scores, axis=0, keepdims=True)
+        weight = jnp.exp(scores - top)
+        total = jnp.sum(weight, axis=0, keepdims=True)
+        weights[by] = weight.astype(jnp.bfloat16)
+        stats_own[by, 0:1, :] = top
+        stats_own[by, 1:2, :] = total
+        stats_own[by, 2:8, :] = jnp.zeros((6, half), jnp.float32)
+
+    order = list(range(1, floors)) + [0]
+    score(0)
+    for by in range(1, floors - 1):
+        score(by)
+    labels_beside.wait_recv()
+    labels_relay = send(lbuf.at[block(2)], lbuf.at[block(3)], twin)
+    score(floors - 1)
+    labels_twin.wait_recv()
+    labels_relay.wait_recv()
+
+    numer_across, stats_across = {}, {}
+    wide = 2 * padded
+    for by in order:
+        numer = lax.dot_general(
+            weights[by], lbuf[...], (((0,), (0,)), ((), ())), preferred_element_type=jnp.float32
+        )
+        low, high = numer[:, :wide], numer[:, wide:]
+        numer_out[by] = jnp.where(x == 0, high, low).astype(jnp.bfloat16)
+        numer_across[by] = send(numer_out.at[by], numer_in.at[by], across)
+        stats_across[by] = send(stats_own.at[by], stats_in.at[by], across)
+        numer_own[by] = jnp.where(x == 0, low, high)
+
+    numer_home, stats_home = {}, {}
+    for by in order:
+        stats_across[by].wait_recv()
+        numer_across[by].wait_recv()
+        top_own, top_in = stats_own[by, 0:1, :], stats_in[by, 0:1, :]
+        top = jnp.maximum(top_own, top_in)
+        carry_own, carry_in = jnp.exp(top_own - top), jnp.exp(top_in - top)
+        total = stats_own[by, 1:2, :] * carry_own + stats_in[by, 1:2, :] * carry_in
+        times = wide // half
+        merged = numer_own[by] * widen(spread(carry_own, half), times) + numer_in[by].astype(
+            jnp.float32
+        ) * widen(spread(carry_in, half), times)
+        home_stats_out[by, 0:1, :] = top
+        home_stats_out[by, 1:2, :] = total
+        home_stats_out[by, 2:8, :] = jnp.zeros((6, half), jnp.float32)
+        if by > 0:
+            home_out[by] = merged.astype(jnp.bfloat16)
+            numer_home[by] = send(home_out.at[by], home_in.at[by], floor_peer(floors - by))
+            stats_home[by] = send(
+                home_stats_out.at[by], home_stats_in.at[by], floor_peer(floors - by)
+            )
+        else:
+            numer_own[0] = merged
+
+    for by in range(1, floors):
+        stats_home[by].wait_recv()
+    tops = [home_stats_out[0, 0:1, :]] + [home_stats_in[by, 0:1, :] for by in range(1, floors)]
+    totals = [home_stats_out[0, 1:2, :]] + [home_stats_in[by, 1:2, :] for by in range(1, floors)]
+    top = functools.reduce(jnp.maximum, tops)
+    carries = [jnp.exp(t - top) for t in tops]
+    total = functools.reduce(jnp.add, [t * c for t, c in zip(totals, carries)])
+    shares = [widen(spread(c / total, half), wide // half) for c in carries]
+    result = numer_own[0] * shares[0]
+    for by in range(1, floors):
+        numer_home[by].wait_recv()
+        result = result + home_in[by].astype(jnp.float32) * shares[by]
+    result = result.astype(jnp.bfloat16)
+    low, high = result[:, :padded], result[:, padded:]
+    final_out[...] = jnp.where(core == 0, high, low)
+    final = send(final_out, final_in, twin)
+    out_ref[mine, :] = jnp.where(core == 0, low, high)[:, :part]
+    final.wait_recv()
+    out_ref[other, :] = final_in[:, :part]
+    for copy in started:
+        copy.wait_send()
+
+
+def plane_body(queries, assign, band_mask, keys, labels, prior):
+    clusters = lax.axis_size("cluster")
+    floors = clusters // 2
+    half, width = queries.shape[0] // 2, queries.shape[1]
+    rows, depth = keys.shape
+    part = labels.shape[1] // 4
+    padded = -(-part // 128) * 128
+    vmem = pl.BlockSpec(memory_space=pltpu.VMEM)
+    bf16, f32 = jnp.bfloat16, jnp.float32
+    copies = 20 + 7 * floors
+    return pl.pallas_call(
+        functools.partial(plane_kernel, temper / math.sqrt(depth)),
+        out_shape=jax.ShapeDtypeStruct((2 * half, part), bf16),
+        in_specs=[vmem, vmem, pl.BlockSpec(memory_space=pltpu.SMEM), vmem, vmem, vmem],
+        out_specs=vmem,
+        scratch_shapes=[
+            pltpu.VMEM((floors, 2, 2, half, width), bf16),
+            pltpu.VMEM((floors, clusters, half), f32),
+            pltpu.VMEM((4 * rows, depth), bf16),
+            pltpu.VMEM((4 * rows, 4 * padded), bf16),
+            pltpu.VMEM((4, 8, rows), f32),
+            pltpu.VMEM((floors, 4 * rows, half), bf16),
+            pltpu.VMEM((floors, 8, half), f32),
+            pltpu.VMEM((floors, half, 2 * padded), f32),
+            pltpu.VMEM((floors, half, 2 * padded), bf16),
+            pltpu.VMEM((floors, half, 2 * padded), bf16),
+            pltpu.VMEM((floors, 8, half), f32),
+            pltpu.VMEM((floors, half, 2 * padded), bf16),
+            pltpu.VMEM((floors, 8, half), f32),
+            pltpu.VMEM((floors, half, 2 * padded), bf16),
+            pltpu.VMEM((floors, 8, half), f32),
+            pltpu.VMEM((half, padded), bf16),
+            pltpu.VMEM((half, padded), bf16),
+            pltpu.SemaphoreType.DMA((copies,)),
+            pltpu.SemaphoreType.DMA((copies,)),
+        ],
+        compiler_params=pltpu.CompilerParams(
+            collective_id=0, has_side_effects=True, vmem_limit_bytes=40 * 1024 * 1024
+        ),
+    )(queries, assign.reshape(1, -1), band_mask, keys, labels, prior.reshape(1, -1))
 
 
 def from_behind(array, axis, by):
@@ -125,4 +411,5 @@
         P(("cluster", "feat")),
     )
     out_specs = P("cluster", "feat")
-    return jax.shard_map(body, mesh=mesh, in_specs=in_specs, out_specs=out_specs, check_vma=False)
+    planes = mesh.shape["cluster"] == 8 and mesh.shape["feat"] == 4
+    return jax.shard_map(plane_body if planes else body, mesh=mesh, in_specs=in_specs, out_specs=out_specs, check_vma=False)

time: 197 us -> 48.7 us (0.25)
  waiting for transfers between devices: 98.1 us -> 0 us
  Pallas kernels: 0 us -> 46.6 us
  starting transfers between devices: 27.1 us -> 0 us
  blocking collectives: 26.4 us -> 0 us
  between operations: 18 us -> 0.06 us
  matrix products: 15.4 us -> 0 us
  local copies, waits for them, and re-layouts: 7.11 us -> 1.84 us
  other arithmetic: 4.02 us -> 0 us
    ppermute x18 -> x0, waiting for transfers between devices: 57.3 us -> none  [from_behind(): lax.ppermute(array, axis, [(i, (i + by) % peers) for i in range(peers)])]
    pallas_call x0 -> x1, Pallas kernels: none -> 46.6 us  [plane_body(): pl.pallas_call(functools.partial(plane_kernel, temper / math.sqrt(depth))...]
    unnamed x3 -> x0, waiting for transfers between devices: 32.3 us -> none
    ppermute x18 -> x0, starting transfers between devices: 21.5 us -> none  [from_behind(): lax.ppermute(array, axis, [(i, (i + by) % peers) for i in range(peers)])]
    all_to_all x1 -> x0, blocking collectives: 16.1 us -> none  [body(): lax.all_to_all(outgoing.reshape(clusters, capacity, queries.shape[1]), 'c...]
    dot_general x14 -> x0, matrix products: 15.4 us -> none  [the longest x7 9.33 us: absorb(): jnp.dot(weight.astype(jnp.bfloat16), block_labels, preferred_element_type...]
    all_gather x2 -> x0, blocking collectives: 10.3 us -> none  [combined_all(): gathered = jax.tree.map(lambda a: lax.all_gather(a, axis), part)]
    all_to_all x1 -> x0, waiting for transfers between devices: 8.52 us -> none  [body(): lax.all_to_all(shares.reshape(clusters, capacity, shares.shape[1]), 'clus...]
  transfers between devices with their start and end apart: 21 -> 0, of which waited for: 11 -> 0; matrix products, arithmetic and copies ran while one was open for 7% -> 0% of each run, Pallas kernels for 0% -> 0%
where the time goes in v1:
time: 48.7 us; the launch traced here: 48.5 us
  Pallas kernels  46.6 us (96%)
  local copies, waits for them, and re-layouts  1.84 us (4%)
    pallas_call x1, Pallas kernels, plane_body(): pl.pallas_call(functools.partial(plane_kernel, temper / math.sqrt(depth))...  46.6 us
    unnamed x12, local copies, waits for them, and re-layouts  1.84 us

profile of v1, /device:TPU:0, one launch (start us, length us, event | category | flops | bytes accessed | tf_op | source)
XLA Modules:
  0.0 48.5 jit_solution(12441904881893836077)
XLA Ops:
  0.0 0.0 copy-start
  0.0 0.0 copy-start.1
  0.0 0.0 copy-start.2
  0.0 0.0 copy-start.3
  0.0 0.0 copy-start.4
  0.0 1.2 %copy.7.labels_ref = bf16[128,1000]{1,0:T(8,128)(2,1)S(1)} copy(bf16[128,1000]{0,1:T(8,128)(2,1)} %param.10) | data formatting | bytes 512000 | tf_op args[4]
  1.2 0.0 copy-done
  1.2 0.0 copy-done.1
  1.2 0.0 copy-done.2
  1.2 0.0 copy-done.3
  1.2 0.0 copy-done.4
  1.2 46.6 %shard_map.64 = bf16[256,250]{1,0:T(8,128)(2,1)S(1)} custom-call(bf16[256,256]{1,0:T(8,128)(2,1)S(1)} %copy-done.1, s32[1,256]{1,0:T(1,128)S(1)} %bitcast.2, s32[8,7]{1,0:T(8,128)S(1)} %copy-done.2, bf16[128,1024]{1,0:T(8,128)(2,1)S(1)} %copy-done, bf16[128,1000]{1,0:T(8,128)(2,1)S(1)} %copy.7.labels_ref, bf16[1,128]{1,0:T(2,128)(2,1)S(1)} %bitcast.3), custom_call_target="tpu_custom_call" | custom-call | tf_op jit(solution)/shard_map/pallas_call | solution.py:268
  47.9 0.7 %copy.9 = bf16[256,250]{1,0:T(8,128)(2,1)} copy(bf16[256,250]{1,0:T(8,128)(2,1)S(1)} %shard_map.64) | data formatting | bytes 256000
Async XLA Ops:
  0.0 1.2 %copy-start = (bf16[128,1024]{1,0:T(8,128)(2,1)S(1)}, bf16[128,1024]{1,0:T(8,128)(2,1)}, u32[]{:S(2)}) copy-start(bf16[128,1024]{1,0:T(8,128)(2,1)} %keys_ref.1) | copy-start | bytes 786436
  0.0 1.2 %copy-start.1 = (bf16[256,256]{1,0:T(8,128)(2,1)S(1)}, bf16[256,256]{1,0:T(8,128)(2,1)}, u32[]{:S(2)}) copy-start(bf16[256,256]{1,0:T(8,128)(2,1)} %queries_ref.1) | copy-start | bytes 393220
  0.0 1.2 %copy-start.2 = (s32[8,7]{1,0:T(8,128)S(1)}, s32[8,7]{1,0:T(8,128)}, u32[]{:S(2)}) copy-start(s32[8,7]{1,0:T(8,128)} %mask_ref.1) | copy-start | bytes 676
  0.0 1.2 %copy-start.3 = (s32[256,1]{0,1:T(1,128)S(1)}, s32[256,1]{0,1:T(1,128)}, u32[]{:S(2)}) copy-start(s32[256,1]{0,1:T(1,128)} %param.7) | copy-start | bytes 3076
  0.0 1.2 %copy-start.4 = (bf16[128]{0:T(256)(128)(2,1)S(1)}, bf16[128]{0:T(256)(128)(2,1)}, u32[]{:S(2)}) copy-start(bf16[128]{0:T(256)(128)(2,1)} %param.11) | copy-start | bytes 772

commit v2 on v1

--- a/solution.py
+++ b/solution.py
@@ -18,10 +18,6 @@
 
 def spread(row, width):
     return jnp.broadcast_to(row, (width, row.shape[1])).T
-
-
-def widen(column, times):
-    return jnp.concatenate([column] * times, axis=1)
 
 
 def plane_kernel(
@@ -52,6 +48,7 @@
     final_in,
     send_sem,
     recv_sem,
+    home_sem,
 ):
     cluster = lax.axis_index("cluster")
     feat = lax.axis_index("feat")
@@ -59,44 +56,70 @@
     floors = clusters // 2
     half = queries_ref.shape[0] // 2
     rows = keys_ref.shape[0]
-    part = labels_ref.shape[1] // 4
-    padded = lbuf.shape[1] // 4
+    part = labels_ref.shape[0] // 4
+    padded = lbuf.shape[2] // 2
     z, y = lax.div(cluster, 2), lax.rem(cluster, 2)
     x, core = lax.div(feat, 2), lax.rem(feat, 2)
     twin = (cluster, feat + 1 - 2 * core)
     across = (cluster, feat + 2 - 4 * x)
     beside = (cluster + 1 - 2 * y, feat)
-
-    def floor_peer(by):
-        return (lax.rem(cluster + 2 * by, clusters), feat)
+    above, below = (cluster + 2, feat), (cluster - 2, feat)
+    MAIN, EXTRA, ACROSS, SEEN, NUMER, STATS = range(6)
+
+    inner = jnp.minimum(z, floors - 1 - z)
+    upper = lax.div(z, 2)
+
+    def home_at(step):
+        if step == 0:
+            return z
+        near = step - inner if step == 1 else step + 0 * inner
+        return near + upper * (floors - 1 - 2 * near)
+
+    homes = [home_at(step) for step in range(floors)]
+
+    def floor_peer(floor):
+        return (2 * floor + y, feat)
 
     barrier = pltpu.get_barrier_semaphore()
-    peers = [twin, across, beside] + [floor_peer(by) for by in range(1, floors)]
+    peers = [twin, across, beside] + [floor_peer(home) for home in homes[1:]]
     for peer in peers:
         pl.semaphore_signal(barrier, inc=1, device_id=peer, device_id_type=MESH)
     pl.semaphore_wait(barrier, len(peers))
 
     started = []
 
-    def send(src, dst, peer):
+    def send(src, dst, peer, where=None, only=None):
         index = len(started)
         copy = pltpu.make_async_remote_copy(
             src_ref=src,
             dst_ref=dst,
             send_sem=send_sem.at[index],
-            recv_sem=recv_sem.at[index],
+            recv_sem=recv_sem.at[index] if where is None else home_sem.at[where[0], where[1]],
             device_id=peer,
             device_id_type=MESH,
         )
-        copy.start()
-        started.append(copy)
+        started.append((copy, only))
+        if only is None:
+            copy.start()
+        else:
+            pl.when(only)(copy.start)
         return copy
+
+    def arrived(ref, kind, index):
+        pltpu.make_async_remote_copy(
+            src_ref=ref,
+            dst_ref=ref,
+            send_sem=send_sem.at[0],
+            recv_sem=home_sem.at[kind, index],
+            device_id=twin,
+            device_id_type=MESH,
+        ).wait_recv()
+
+    mine = pl.ds(pl.multiple_of(core * half, half), half)
+    other = pl.ds(pl.multiple_of((1 - core) * half, half), half)
 
     def block(index):
         return pl.ds(index * rows, rows)
-
-    mine = pl.ds(pl.multiple_of(core * half, half), half)
-    other = pl.ds(pl.multiple_of((1 - core) * half, half), half)
 
     query_twin = send(queries_ref.at[other], qbuf.at[z, x, core], twin)
     keys_beside = send(keys_ref, kbuf.at[block(2)], beside)
@@ -105,6 +128,23 @@
     keys_twin = send(keys_ref, kbuf.at[block(1)], twin)
     prior_twin = send(pbuf.at[0], pbuf.at[1], twin)
     qbuf[z, x, core] = queries_ref[mine, :]
+
+    def pass_on(home, kind, piece):
+        send(piece, piece, above, (kind, home), (home <= z) & (z < floors - 1))
+        send(piece, piece, below, (kind, home), (home >= z) & (z > 0))
+
+    query_twin.wait_recv()
+    pass_on(z, MAIN, qbuf.at[z, x])
+    query_across = send(qbuf.at[z, x], qbuf.at[z, x], across)
+
+    lbuf[0] = jnp.zeros(lbuf.shape[1:], lbuf.dtype)
+    for quarter in range(4):
+        start = (quarter % 2) * padded
+        lbuf[0, quarter // 2, start : start + part, :] = labels_ref[
+            quarter * part : (quarter + 1) * part, :
+        ]
+    labels_beside = [send(lbuf.at[0, side], lbuf.at[2, side], beside) for side in (1 - x, x)]
+    labels_twin = [send(lbuf.at[0, side], lbuf.at[1, side], twin) for side in (1 - x, x)]
 
     assigned = assign_ref[...]
     assigned = jnp.where(core == 0, assigned[:, :half], assigned[:, half:])
@@ -119,58 +159,35 @@
             )
         seen = jnp.where(assigned == owner, column, seen)
     vbuf[z] = jnp.where(seen > 0, jnp.float32(0.0), jnp.float32(HIDDEN))
-    seen_floor = [None] + [send(vbuf.at[z], vbuf.at[z], floor_peer(by)) for by in range(1, floors)]
-
-    query_twin.wait_recv()
-    query_floor = [None] + [
-        send(qbuf.at[z, x], qbuf.at[z, x], floor_peer(by)) for by in range(1, floors)
-    ]
-    query_across = [send(qbuf.at[z, x], qbuf.at[z, x], across)]
-
-    lbuf[block(0), :] = jnp.zeros((rows, 4 * padded), lbuf.dtype)
-    for quarter in range(4):
-        lbuf[block(0), quarter * padded : quarter * padded + part] = labels_ref[
-            :, quarter * part : (quarter + 1) * part
-        ]
-    labels_beside = send(lbuf.at[block(0)], lbuf.at[block(2)], beside)
-    labels_twin = send(lbuf.at[block(0)], lbuf.at[block(1)], twin)
+    for home in homes[1:]:
+        send(vbuf.at[z], vbuf.at[z], floor_peer(home), (SEEN, z))
     kbuf[block(0), :] = keys_ref[...]
 
-    def home(by):
-        return lax.rem(z - by + floors, floors)
-
-    def forward_query(by):
-        query_floor[by].wait_recv()
-        source = home(by)
-        query_across.append(send(qbuf.at[source, x], qbuf.at[source, x], across))
-
-    forward_query(1)
-    keys_beside.wait_recv()
-    prior_beside.wait_recv()
-    keys_relay = send(kbuf.at[block(2)], kbuf.at[block(3)], twin)
-    prior_relay = send(pbuf.at[2], pbuf.at[3], twin)
-    for by in range(2, floors):
-        forward_query(by)
-    for copy in (keys_twin, prior_twin, keys_relay, prior_relay):
-        copy.wait_recv()
-
-    def score(by):
-        source = home(by)
-        query_across[by].wait_recv()
-        if by > 0:
-            seen_floor[by].wait_recv()
+    def relay(step):
+        home = homes[step]
+        arrived(qbuf.at[home, x], MAIN, home)
+        pass_on(home, MAIN, qbuf.at[home, x])
+        send(qbuf.at[home, x, 0], qbuf.at[home, x, 0], across, (ACROSS, home))
+        arrived(qbuf.at[home, 1 - x, 1], EXTRA, home)
+        pass_on(home, EXTRA, qbuf.at[home, 1 - x, 1])
+
+    def score(step):
+        home = homes[step]
+        if step > 0:
+            arrived(qbuf.at[home, 1 - x, 0], ACROSS, home)
+            arrived(vbuf.at[home], SEEN, home)
         width = qbuf.shape[4]
         scores = jnp.zeros((4 * rows, half), jnp.float32)
         for quarter in range(4):
             scores = scores + lax.dot_general(
                 kbuf[:, quarter * width : (quarter + 1) * width],
-                qbuf[source, quarter // 2, quarter % 2],
+                qbuf[home, quarter // 2, quarter % 2],
                 (((1,), (1,)), ((), ())),
                 preferred_element_type=jnp.float32,
             )
         scores = scores * scale
-        near = vbuf[source, pl.ds(cluster, 1), :]
-        far = vbuf[source, pl.ds(cluster + 1 - 2 * y, 1), :]
+        near = vbuf[home, pl.ds(cluster, 1), :]
+        far = vbuf[home, pl.ds(cluster + 1 - 2 * y, 1), :]
         pieces = []
         for index in range(4):
             bias = spread(pbuf[index, 0:1, :], half)
@@ -181,78 +198,93 @@
         top = jnp.max(scores, axis=0, keepdims=True)
         weight = jnp.exp(scores - top)
         total = jnp.sum(weight, axis=0, keepdims=True)
-        weights[by] = weight.astype(jnp.bfloat16)
-        stats_own[by, 0:1, :] = top
-        stats_own[by, 1:2, :] = total
-        stats_own[by, 2:8, :] = jnp.zeros((6, half), jnp.float32)
-
-    order = list(range(1, floors)) + [0]
+        weights[step] = weight.astype(jnp.bfloat16)
+        stats_own[step, 0:1, :] = top
+        stats_own[step, 1:2, :] = total
+        stats_own[step, 2:8, :] = jnp.zeros((6, half), jnp.float32)
+
+    def class_sum(step, side):
+        blocks = jnp.concatenate([lbuf[index, side] for index in range(4)], axis=1)
+        return jnp.dot(blocks, weights[step], preferred_element_type=jnp.float32)
+
+    numer_across, stats_across = {}, {}
+
+    def send_across(step):
+        numer_out[step] = class_sum(step, 1 - x).astype(jnp.bfloat16)
+        stats_across[step] = send(stats_own.at[step], stats_in.at[step], across)
+        numer_across[step] = send(numer_out.at[step], numer_in.at[step], across)
+
+    query_across.wait_recv()
+    pass_on(z, EXTRA, qbuf.at[z, 1 - x, 1])
+    relay(1)
+    keys_beside.wait_recv()
+    prior_beside.wait_recv()
+    keys_relay = send(kbuf.at[block(2)], kbuf.at[block(3)], twin)
+    prior_relay = send(pbuf.at[2], pbuf.at[3], twin)
+    relay(2)
+    for copy in (keys_twin, prior_twin, keys_relay, prior_relay):
+        copy.wait_recv()
     score(0)
-    for by in range(1, floors - 1):
-        score(by)
-    labels_beside.wait_recv()
-    labels_relay = send(lbuf.at[block(2)], lbuf.at[block(3)], twin)
-    score(floors - 1)
-    labels_twin.wait_recv()
-    labels_relay.wait_recv()
-
-    numer_across, stats_across = {}, {}
-    wide = 2 * padded
-    for by in order:
-        numer = lax.dot_general(
-            weights[by], lbuf[...], (((0,), (0,)), ((), ())), preferred_element_type=jnp.float32
-        )
-        low, high = numer[:, :wide], numer[:, wide:]
-        numer_out[by] = jnp.where(x == 0, high, low).astype(jnp.bfloat16)
-        numer_across[by] = send(numer_out.at[by], numer_in.at[by], across)
-        stats_across[by] = send(stats_own.at[by], stats_in.at[by], across)
-        numer_own[by] = jnp.where(x == 0, low, high)
-
-    numer_home, stats_home = {}, {}
-    for by in order:
-        stats_across[by].wait_recv()
-        numer_across[by].wait_recv()
-        top_own, top_in = stats_own[by, 0:1, :], stats_in[by, 0:1, :]
+    relay(3)
+    score(1)
+    labels_beside[0].wait_recv()
+    labels_relay = [send(lbuf.at[2, 1 - x], lbuf.at[3, 1 - x], twin)]
+    score(2)
+    labels_twin[0].wait_recv()
+    labels_relay[0].wait_recv()
+    send_across(1)
+    send_across(2)
+    labels_beside[1].wait_recv()
+    labels_relay.append(send(lbuf.at[2, x], lbuf.at[3, x], twin))
+    score(3)
+    send_across(3)
+    send_across(0)
+    labels_twin[1].wait_recv()
+    labels_relay[1].wait_recv()
+
+    for step in (1, 2, 3, 0):
+        numer_own[step] = class_sum(step, x)
+        stats_across[step].wait_recv()
+        numer_across[step].wait_recv()
+        top_own, top_in = stats_own[step, 0:1, :], stats_in[step, 0:1, :]
         top = jnp.maximum(top_own, top_in)
         carry_own, carry_in = jnp.exp(top_own - top), jnp.exp(top_in - top)
-        total = stats_own[by, 1:2, :] * carry_own + stats_in[by, 1:2, :] * carry_in
-        times = wide // half
-        merged = numer_own[by] * widen(spread(carry_own, half), times) + numer_in[by].astype(
-            jnp.float32
-        ) * widen(spread(carry_in, half), times)
-        home_stats_out[by, 0:1, :] = top
-        home_stats_out[by, 1:2, :] = total
-        home_stats_out[by, 2:8, :] = jnp.zeros((6, half), jnp.float32)
-        if by > 0:
-            home_out[by] = merged.astype(jnp.bfloat16)
-            numer_home[by] = send(home_out.at[by], home_in.at[by], floor_peer(floors - by))
-            stats_home[by] = send(
-                home_stats_out.at[by], home_stats_in.at[by], floor_peer(floors - by)
-            )
+        total = stats_own[step, 1:2, :] * carry_own + stats_in[step, 1:2, :] * carry_in
+        merged = numer_own[step] * carry_own + numer_in[step].astype(jnp.float32) * carry_in
+        home_stats_out[step, 0:1, :] = top
+        home_stats_out[step, 1:2, :] = total
+        home_stats_out[step, 2:8, :] = jnp.zeros((6, half), jnp.float32)
+        if step > 0:
+            home_out[step] = merged.astype(jnp.bfloat16)
+            peer = floor_peer(homes[step])
+            send(home_stats_out.at[step], home_stats_in.at[z], peer, (STATS, z))
+            send(home_out.at[step], home_in.at[z], peer, (NUMER, z))
         else:
             numer_own[0] = merged
 
-    for by in range(1, floors):
-        stats_home[by].wait_recv()
-    tops = [home_stats_out[0, 0:1, :]] + [home_stats_in[by, 0:1, :] for by in range(1, floors)]
-    totals = [home_stats_out[0, 1:2, :]] + [home_stats_in[by, 1:2, :] for by in range(1, floors)]
+    for home in homes[1:]:
+        arrived(home_stats_in.at[home], STATS, home)
+    tops = [home_stats_out[0, 0:1, :]] + [home_stats_in[home, 0:1, :] for home in homes[1:]]
+    totals = [home_stats_out[0, 1:2, :]] + [home_stats_in[home, 1:2, :] for home in homes[1:]]
     top = functools.reduce(jnp.maximum, tops)
     carries = [jnp.exp(t - top) for t in tops]
     total = functools.reduce(jnp.add, [t * c for t, c in zip(totals, carries)])
-    shares = [widen(spread(c / total, half), wide // half) for c in carries]
-    result = numer_own[0] * shares[0]
-    for by in range(1, floors):
-        numer_home[by].wait_recv()
-        result = result + home_in[by].astype(jnp.float32) * shares[by]
-    result = result.astype(jnp.bfloat16)
-    low, high = result[:, :padded], result[:, padded:]
+    result = numer_own[0] * (carries[0] / total)
+    for step in range(1, floors):
+        home = homes[step]
+        arrived(home_in.at[home], NUMER, home)
+        result = result + home_in[home].astype(jnp.float32) * (carries[step] / total)
+    low, high = result[:padded].T.astype(jnp.bfloat16), result[padded:].T.astype(jnp.bfloat16)
     final_out[...] = jnp.where(core == 0, high, low)
     final = send(final_out, final_in, twin)
     out_ref[mine, :] = jnp.where(core == 0, low, high)[:, :part]
     final.wait_recv()
     out_ref[other, :] = final_in[:, :part]
-    for copy in started:
-        copy.wait_send()
+    for copy, only in started:
+        if only is None:
+            copy.wait_send()
+        else:
+            pl.when(only)(copy.wait_send)
 
 
 def plane_body(queries, assign, band_mask, keys, labels, prior):
@@ -264,7 +296,7 @@
     padded = -(-part // 128) * 128
     vmem = pl.BlockSpec(memory_space=pltpu.VMEM)
     bf16, f32 = jnp.bfloat16, jnp.float32
-    copies = 20 + 7 * floors
+    copies = 64
     return pl.pallas_call(
         functools.partial(plane_kernel, temper / math.sqrt(depth)),
         out_shape=jax.ShapeDtypeStruct((2 * half, part), bf16),
@@ -274,27 +306,28 @@
             pltpu.VMEM((floors, 2, 2, half, width), bf16),
             pltpu.VMEM((floors, clusters, half), f32),
             pltpu.VMEM((4 * rows, depth), bf16),
-            pltpu.VMEM((4 * rows, 4 * padded), bf16),
+            pltpu.VMEM((4, 2, 2 * padded, rows), bf16),
             pltpu.VMEM((4, 8, rows), f32),
             pltpu.VMEM((floors, 4 * rows, half), bf16),
             pltpu.VMEM((floors, 8, half), f32),
-            pltpu.VMEM((floors, half, 2 * padded), f32),
-            pltpu.VMEM((floors, half, 2 * padded), bf16),
-            pltpu.VMEM((floors, half, 2 * padded), bf16),
+            pltpu.VMEM((floors, 2 * padded, half), f32),
+            pltpu.VMEM((floors, 2 * padded, half), bf16),
+            pltpu.VMEM((floors, 2 * padded, half), bf16),
             pltpu.VMEM((floors, 8, half), f32),
-            pltpu.VMEM((floors, half, 2 * padded), bf16),
+            pltpu.VMEM((floors, 2 * padded, half), bf16),
             pltpu.VMEM((floors, 8, half), f32),
-            pltpu.VMEM((floors, half, 2 * padded), bf16),
+            pltpu.VMEM((floors, 2 * padded, half), bf16),
             pltpu.VMEM((floors, 8, half), f32),
             pltpu.VMEM((half, padded), bf16),
             pltpu.VMEM((half, padded), bf16),
             pltpu.SemaphoreType.DMA((copies,)),
             pltpu.SemaphoreType.DMA((copies,)),
+            pltpu.SemaphoreType.DMA((6, floors)),
         ],
         compiler_params=pltpu.CompilerParams(
             collective_id=0, has_side_effects=True, vmem_limit_bytes=40 * 1024 * 1024
         ),
-    )(queries, assign.reshape(1, -1), band_mask, keys, labels, prior.reshape(1, -1))
+    )(queries, assign.reshape(1, -1), band_mask, keys, labels.T, prior.reshape(1, -1))
 
 
 def from_behind(array, axis, by):

time: 48.7 us -> 50 us (1.027)
  local copies, waits for them, and re-layouts: 1.84 us -> 4.15 us
  Pallas kernels: 46.6 us -> 45.6 us
    unnamed x12 -> x13, local copies, waits for them, and re-layouts: 1.84 us -> 4.15 us
    pallas_call x1, Pallas kernels: 46.6 us -> 45.6 us  [plane_body(): pl.pallas_call(functools.partial(plane_kernel, temper / math.sqrt(depth))...]
where the time goes in v2:
time: 50 us; the launch traced here: 49.8 us
  Pallas kernels  45.6 us (91%)
  local copies, waits for them, and re-layouts  4.15 us (8%)
    pallas_call x1, Pallas kernels, plane_body(): pl.pallas_call(functools.partial(plane_kernel, temper / math.sqrt(depth))...  45.6 us
    unnamed x13, local copies, waits for them, and re-layouts  4.15 us

profile of v2, /device:TPU:0, one launch (start us, length us, event | category | flops | bytes accessed | tf_op | source)
XLA Modules:
  0.0 49.8 jit_solution(12929090937401712799)
XLA Ops:
  0.0 0.0 copy-start.3
  0.0 0.0 copy-start.4
  0.0 0.0 copy-start.5
  0.0 0.7 %copy-done.3 = s32[8,7]{1,0:T(8,128)S(1)} copy-done((s32[8,7]{1,0:T(8,128)S(1)}, s32[8,7]{1,0:T(8,128)}, u32[]{:S(2)}) %copy-start.3) | copy-done | bytes 248
  0.7 0.0 copy-done.4
  0.7 0.0 copy-done.5
  0.7 0.0 copy-start
  0.7 0.9 %copy-done = bf16[128,1024]{1,0:T(8,128)(2,1)S(1)} copy-done((bf16[128,1024]{1,0:T(8,128)(2,1)S(1)}, bf16[128,1024]{1,0:T(8,128)(2,1)}, u32[]{:S(2)}) %copy-start) | copy-done | bytes 262168
  1.6 0.0 copy-start.1
  1.7 0.9 %copy-done.1 = bf16[128,1000]{0,1:T(8,128)(2,1)S(1)} copy-done((bf16[128,1000]{0,1:T(8,128)(2,1)S(1)}, bf16[128,1000]{0,1:T(8,128)(2,1)}, u32[]{:S(2)}) %copy-start.1) | copy-done | bytes 256024
  2.6 0.0 copy-start.2
  2.6 0.9 %copy-done.2 = bf16[256,256]{1,0:T(8,128)(2,1)S(1)} copy-done((bf16[256,256]{1,0:T(8,128)(2,1)S(1)}, bf16[256,256]{1,0:T(8,128)(2,1)}, u32[]{:S(2)}) %copy-start.2) | copy-done | bytes 131096
  3.5 45.6 %shard_map.64 = bf16[256,250]{1,0:T(8,128)(2,1)S(1)} custom-call(bf16[256,256]{1,0:T(8,128)(2,1)S(1)} %copy-done.2, s32[1,256]{1,0:T(1,128)S(1)} %bitcast.4, s32[8,7]{1,0:T(8,128)S(1)} %copy-done.3, bf16[128,1024]{1,0:T(8,128)(2,1)S(1)} %copy-done, bf16[1000,128]{1,0:T(8,128)(2,1)S(1)} %bitcast.3, bf16[1,128]{1,0:T(2,128)(2,1)S(1)} %bitcast.5), custom_call_target="tpu_custom_call" | custom-call | tf_op jit(solution)/shard_map/pallas_call | solution.py:300
  49.1 0.7 %copy.8 = bf16[256,250]{1,0:T(8,128)(2,1)} copy(bf16[256,250]{1,0:T(8,128)(2,1)S(1)} %shard_map.64) | data formatting | bytes 256000
Async XLA Ops:
  0.0 0.7 %copy-start.3 = (s32[8,7]{1,0:T(8,128)S(1)}, s32[8,7]{1,0:T(8,128)}, u32[]{:S(2)}) copy-start(s32[8,7]{1,0:T(8,128)} %mask_ref.1) | copy-start | bytes 676
  0.0 0.7 %copy-start.4 = (s32[256,1]{0,1:T(1,128)S(1)}, s32[256,1]{0,1:T(1,128)}, u32[]{:S(2)}) copy-start(s32[256,1]{0,1:T(1,128)} %param.7) | copy-start | bytes 3076
  0.0 0.7 %copy-start.5 = (bf16[128]{0:T(256)(128)(2,1)S(1)}, bf16[128]{0:T(256)(128)(2,1)}, u32[]{:S(2)}) copy-start(bf16[128]{0:T(256)(128)(2,1)} %param.11) | copy-start | bytes 772
  0.7 1.0 %copy-start = (bf16[128,1024]{1,0:T(8,128)(2,1)S(1)}, bf16[128,1024]{1,0:T(8,128)(2,1)}, u32[]{:S(2)}) copy-start(bf16[128,1024]{1,0:T(8,128)(2,1)} %keys_ref.1) | copy-start | bytes 786436
  1.6 0.9 %copy-start.1 = (bf16[128,1000]{0,1:T(8,128)(2,1)S(1)}, bf16[128,1000]{0,1:T(8,128)(2,1)}, u32[]{:S(2)}) copy-start(bf16[128,1000]{0,1:T(8,128)(2,1)} %param.10) | copy-start | bytes 768004
  2.6 0.9 %copy-start.2 = (bf16[256,256]{1,0:T(8,128)(2,1)S(1)}, bf16[256,256]{1,0:T(8,128)(2,1)}, u32[]{:S(2)}) copy-start(bf16[256,256]{1,0:T(8,128)(2,1)} %queries_ref.1) | copy-start | bytes 393220

commit v3 on v2

--- a/solution.py
+++ b/solution.py
@@ -29,11 +29,16 @@
     labels_ref,
     prior_ref,
     out_ref,
+    assign_buf,
+    mask_buf,
+    prior_buf,
+    labels_buf,
     qbuf,
     vbuf,
     kbuf,
     lbuf,
     pbuf,
+    bias,
     weights,
     stats_own,
     numer_own,
@@ -44,11 +49,10 @@
     home_stats_out,
     home_in,
     home_stats_in,
-    final_out,
-    final_in,
     send_sem,
     recv_sem,
     home_sem,
+    load_sem,
 ):
     cluster = lax.axis_index("cluster")
     feat = lax.axis_index("feat")
@@ -63,8 +67,28 @@
     twin = (cluster, feat + 1 - 2 * core)
     across = (cluster, feat + 2 - 4 * x)
     beside = (cluster + 1 - 2 * y, feat)
+
+    def mate(peer):
+        return (peer[0], peer[1] + 1 - 2 * core)
+
     above, below = (cluster + 2, feat), (cluster - 2, feat)
-    MAIN, EXTRA, ACROSS, SEEN, NUMER, STATS = range(6)
+    FIRST, SECOND, EXTRA, ACROSS, SEEN, NUMER, STATS = range(7)
+
+    loads = [
+        pltpu.make_async_copy(src, dst, load_sem.at[index])
+        for index, (src, dst) in enumerate(
+            [
+                (queries_ref.at[pl.ds(core * half, half)], qbuf.at[z, x, core]),
+                (prior_ref, prior_buf),
+                (labels_ref, labels_buf),
+                (mask_ref, mask_buf),
+                (assign_ref, assign_buf),
+                (keys_ref, kbuf.at[pl.ds(0, rows)]),
+            ]
+        )
+    ]
+    for load in loads:
+        load.start()
 
     inner = jnp.minimum(z, floors - 1 - z)
     upper = lax.div(z, 2)
@@ -81,7 +105,9 @@
         return (2 * floor + y, feat)
 
     barrier = pltpu.get_barrier_semaphore()
-    peers = [twin, across, beside] + [floor_peer(home) for home in homes[1:]]
+    peers = [twin, across, mate(across), beside]
+    for home in homes[1:]:
+        peers += [floor_peer(home), mate(floor_peer(home))]
     for peer in peers:
         pl.semaphore_signal(barrier, inc=1, device_id=peer, device_id_type=MESH)
     pl.semaphore_wait(barrier, len(peers))
@@ -117,36 +143,43 @@
 
     mine = pl.ds(pl.multiple_of(core * half, half), half)
     other = pl.ds(pl.multiple_of((1 - core) * half, half), half)
+    up, down = z < floors - 1, z > 0
 
     def block(index):
         return pl.ds(index * rows, rows)
 
-    query_twin = send(queries_ref.at[other], qbuf.at[z, x, core], twin)
+    own, piece = qbuf.at[z, x, core], core
+    query_twin = send(queries_ref.at[other], own, twin)
+    send(queries_ref.at[mine], own, above, (FIRST + piece, z), up)
+    send(queries_ref.at[mine], own, below, (FIRST + piece, z), down)
+    send(queries_ref.at[other], own, mate(above), (FIRST + piece, z), up)
+    send(queries_ref.at[other], own, mate(below), (FIRST + piece, z), down)
+    send(queries_ref.at[mine], own, across, (FIRST + piece, z))
+    send(queries_ref.at[other], own, mate(across), (FIRST + piece, z))
     keys_beside = send(keys_ref, kbuf.at[block(2)], beside)
-    pbuf[0] = jnp.broadcast_to(prior_ref[...].astype(jnp.float32), (8, rows))
+    keys_twin = send(keys_ref, kbuf.at[block(1)], twin)
+    loads[1].wait()
+    pbuf[0] = jnp.broadcast_to(prior_buf[...].astype(jnp.float32), (8, rows))
     prior_beside = send(pbuf.at[0], pbuf.at[2], beside)
-    keys_twin = send(keys_ref, kbuf.at[block(1)], twin)
     prior_twin = send(pbuf.at[0], pbuf.at[1], twin)
-    qbuf[z, x, core] = queries_ref[mine, :]
-
-    def pass_on(home, kind, piece):
-        send(piece, piece, above, (kind, home), (home <= z) & (z < floors - 1))
-        send(piece, piece, below, (kind, home), (home >= z) & (z > 0))
-
-    query_twin.wait_recv()
-    pass_on(z, MAIN, qbuf.at[z, x])
-    query_across = send(qbuf.at[z, x], qbuf.at[z, x], across)
+
+    def pass_on(home, kind, ref, start=False):
+        send(ref, ref, above, (kind, home), (home <= z if start else home < z) & up)
+        send(ref, ref, below, (kind, home), (home >= z if start else home > z) & down)
 
     lbuf[0] = jnp.zeros(lbuf.shape[1:], lbuf.dtype)
+    loads[2].wait()
     for quarter in range(4):
         start = (quarter % 2) * padded
-        lbuf[0, quarter // 2, start : start + part, :] = labels_ref[
+        lbuf[0, quarter // 2, start : start + part, :] = labels_buf[
             quarter * part : (quarter + 1) * part, :
         ]
     labels_beside = [send(lbuf.at[0, side], lbuf.at[2, side], beside) for side in (1 - x, x)]
     labels_twin = [send(lbuf.at[0, side], lbuf.at[1, side], twin) for side in (1 - x, x)]
 
-    assigned = assign_ref[...]
+    loads[3].wait()
+    loads[4].wait()
+    assigned = assign_buf[...]
     assigned = jnp.where(core == 0, assigned[:, :half], assigned[:, half:])
     assigned = jnp.broadcast_to(assigned, (clusters, half))
     row = lax.broadcasted_iota(jnp.int32, (clusters, half), 0)
@@ -155,21 +188,23 @@
         column = jnp.zeros((clusters, half), jnp.int32)
         for step in range(2 * REACH + 1):
             column = jnp.where(
-                row == (owner + step - REACH) % clusters, mask_ref[owner, step], column
+                row == (owner + step - REACH) % clusters, mask_buf[owner, step], column
             )
         seen = jnp.where(assigned == owner, column, seen)
     vbuf[z] = jnp.where(seen > 0, jnp.float32(0.0), jnp.float32(HIDDEN))
     for home in homes[1:]:
         send(vbuf.at[z], vbuf.at[z], floor_peer(home), (SEEN, z))
-    kbuf[block(0), :] = keys_ref[...]
 
     def relay(step):
         home = homes[step]
-        arrived(qbuf.at[home, x], MAIN, home)
-        pass_on(home, MAIN, qbuf.at[home, x])
-        send(qbuf.at[home, x, 0], qbuf.at[home, x, 0], across, (ACROSS, home))
-        arrived(qbuf.at[home, 1 - x, 1], EXTRA, home)
-        pass_on(home, EXTRA, qbuf.at[home, 1 - x, 1])
+        first, second, extra = qbuf.at[home, x, 0], qbuf.at[home, x, 1], qbuf.at[home, 1 - x, 1]
+        arrived(first, FIRST, home)
+        pass_on(home, FIRST, first)
+        send(first, first, across, (ACROSS, home))
+        arrived(second, SECOND, home)
+        pass_on(home, SECOND, second)
+        arrived(extra, EXTRA, home)
+        pass_on(home, EXTRA, extra)
 
     def score(step):
         home = homes[step]
@@ -190,10 +225,8 @@
         far = vbuf[home, pl.ds(cluster + 1 - 2 * y, 1), :]
         pieces = []
         for index in range(4):
-            bias = spread(pbuf[index, 0:1, :], half)
-            pieces.append(
-                scores[index * rows : (index + 1) * rows] + bias + (near if index < 2 else far)
-            )
+            cut = slice(index * rows, (index + 1) * rows)
+            pieces.append(scores[cut] + bias[cut, :] + (near if index < 2 else far))
         scores = jnp.concatenate(pieces, axis=0)
         top = jnp.max(scores, axis=0, keepdims=True)
         weight = jnp.exp(scores - top)
@@ -214,16 +247,21 @@
         stats_across[step] = send(stats_own.at[step], stats_in.at[step], across)
         numer_across[step] = send(numer_out.at[step], numer_in.at[step], across)
 
-    query_across.wait_recv()
-    pass_on(z, EXTRA, qbuf.at[z, 1 - x, 1])
+    arrived(qbuf.at[z, 1 - x, 0], FIRST, z)
+    arrived(qbuf.at[z, 1 - x, 1], SECOND, z)
+    pass_on(z, EXTRA, qbuf.at[z, 1 - x, 1], True)
     relay(1)
     keys_beside.wait_recv()
     prior_beside.wait_recv()
     keys_relay = send(kbuf.at[block(2)], kbuf.at[block(3)], twin)
     prior_relay = send(pbuf.at[2], pbuf.at[3], twin)
     relay(2)
-    for copy in (keys_twin, prior_twin, keys_relay, prior_relay):
+    for copy in (keys_twin, prior_twin, keys_relay, prior_relay, query_twin):
         copy.wait_recv()
+    loads[0].wait()
+    loads[5].wait()
+    for index in range(4):
+        bias[block(index), :] = spread(pbuf[index, 0:1, :], half)
     score(0)
     relay(3)
     score(1)
@@ -254,32 +292,36 @@
         home_stats_out[step, 0:1, :] = top
         home_stats_out[step, 1:2, :] = total
         home_stats_out[step, 2:8, :] = jnp.zeros((6, half), jnp.float32)
+        home_out[step, 0] = merged[:padded].astype(jnp.bfloat16)
+        home_out[step, 1] = merged[padded:].astype(jnp.bfloat16)
+        place = 2 * z + core
+        peer = floor_peer(homes[step])
         if step > 0:
-            home_out[step] = merged.astype(jnp.bfloat16)
-            peer = floor_peer(homes[step])
-            send(home_stats_out.at[step], home_stats_in.at[z], peer, (STATS, z))
-            send(home_out.at[step], home_in.at[z], peer, (NUMER, z))
+            send(home_stats_out.at[step], home_stats_in.at[place], peer, (STATS, place))
+            send(home_out.at[step, core], home_in.at[place], peer, (NUMER, place))
         else:
-            numer_own[0] = merged
-
-    for home in homes[1:]:
-        arrived(home_stats_in.at[home], STATS, home)
-    tops = [home_stats_out[0, 0:1, :]] + [home_stats_in[home, 0:1, :] for home in homes[1:]]
-    totals = [home_stats_out[0, 1:2, :]] + [home_stats_in[home, 1:2, :] for home in homes[1:]]
-    top = functools.reduce(jnp.maximum, tops)
-    carries = [jnp.exp(t - top) for t in tops]
-    total = functools.reduce(jnp.add, [t * c for t, c in zip(totals, carries)])
-    result = numer_own[0] * (carries[0] / total)
-    for step in range(1, floors):
-        home = homes[step]
-        arrived(home_in.at[home], NUMER, home)
-        result = result + home_in[home].astype(jnp.float32) * (carries[step] / total)
-    low, high = result[:padded].T.astype(jnp.bfloat16), result[padded:].T.astype(jnp.bfloat16)
-    final_out[...] = jnp.where(core == 0, high, low)
-    final = send(final_out, final_in, twin)
-    out_ref[mine, :] = jnp.where(core == 0, low, high)[:, :part]
-    final.wait_recv()
-    out_ref[other, :] = final_in[:, :part]
+            home_stats_in[place] = home_stats_out[0]
+            home_in[place] = home_out[0, core]
+        send(home_stats_out.at[step], home_stats_in.at[place], mate(peer), (STATS, place))
+        send(home_out.at[step, 1 - core], home_in.at[place], mate(peer), (NUMER, place))
+
+    for side in (0, 1):
+        source = core if side == 0 else 1 - core
+        places = [2 * home + source for home in homes]
+        for step in range(floors):
+            if side + step > 0:
+                arrived(home_stats_in.at[places[step]], STATS, places[step])
+        tops = [home_stats_in[place, 0:1, :] for place in places]
+        totals = [home_stats_in[place, 1:2, :] for place in places]
+        top = functools.reduce(jnp.maximum, tops)
+        carries = [jnp.exp(t - top) for t in tops]
+        total = functools.reduce(jnp.add, [t * c for t, c in zip(totals, carries)])
+        result = jnp.zeros((padded, half), jnp.float32)
+        for step in range(floors):
+            if side + step > 0:
+                arrived(home_in.at[places[step]], NUMER, places[step])
+            result = result + home_in[places[step]].astype(jnp.float32) * (carries[step] / total)
+        out_ref[mine if side == 0 else other, :] = result.T.astype(jnp.bfloat16)[:, :part]
     for copy, only in started:
         if only is None:
             copy.wait_send()
@@ -296,36 +338,40 @@
     padded = -(-part // 128) * 128
     vmem = pl.BlockSpec(memory_space=pltpu.VMEM)
     bf16, f32 = jnp.bfloat16, jnp.float32
-    copies = 64
+    copies = 80
     return pl.pallas_call(
         functools.partial(plane_kernel, temper / math.sqrt(depth)),
         out_shape=jax.ShapeDtypeStruct((2 * half, part), bf16),
-        in_specs=[vmem, vmem, pl.BlockSpec(memory_space=pltpu.SMEM), vmem, vmem, vmem],
+        in_specs=[pl.BlockSpec(memory_space=pltpu.HBM)] * 6,
         out_specs=vmem,
         scratch_shapes=[
+            pltpu.VMEM((1, 2 * half), jnp.int32),
+            pltpu.SMEM(band_mask.shape, jnp.int32),
+            pltpu.VMEM((1, rows), bf16),
+            pltpu.VMEM((4 * part, rows), bf16),
             pltpu.VMEM((floors, 2, 2, half, width), bf16),
             pltpu.VMEM((floors, clusters, half), f32),
             pltpu.VMEM((4 * rows, depth), bf16),
             pltpu.VMEM((4, 2, 2 * padded, rows), bf16),
             pltpu.VMEM((4, 8, rows), f32),
+            pltpu.VMEM((4 * rows, half), f32),
             pltpu.VMEM((floors, 4 * rows, half), bf16),
             pltpu.VMEM((floors, 8, half), f32),
             pltpu.VMEM((floors, 2 * padded, half), f32),
             pltpu.VMEM((floors, 2 * padded, half), bf16),
             pltpu.VMEM((floors, 2 * padded, half), bf16),
             pltpu.VMEM((floors, 8, half), f32),
-            pltpu.VMEM((floors, 2 * padded, half), bf16),
+            pltpu.VMEM((floors, 2, padded, half), bf16),
             pltpu.VMEM((floors, 8, half), f32),
-            pltpu.VMEM((floors, 2 * padded, half), bf16),
-            pltpu.VMEM((floors, 8, half), f32),
-            pltpu.VMEM((half, padded), bf16),
-            pltpu.VMEM((half, padded), bf16),
+            pltpu.VMEM((2 * floors, padded, half), bf16),
+            pltpu.VMEM((2 * floors, 8, half), f32),
             pltpu.SemaphoreType.DMA((copies,)),
             pltpu.SemaphoreType.DMA((copies,)),
-            pltpu.SemaphoreType.DMA((6, floors)),
+            pltpu.SemaphoreType.DMA((7, 2 * floors)),
+            pltpu.SemaphoreType.DMA((6,)),
         ],
         compiler_params=pltpu.CompilerParams(
-            collective_id=0, has_side_effects=True, vmem_limit_bytes=40 * 1024 * 1024
+            collective_id=0, has_side_effects=True, vmem_limit_bytes=60 * 1024 * 1024
         ),
     )(queries, assign.reshape(1, -1), band_mask, keys, labels.T, prior.reshape(1, -1))
 

time: 50 us -> 46.4 us (0.928)
  local copies, waits for them, and re-layouts: 4.15 us -> 1.57 us
  Pallas kernels: 45.6 us -> 44.6 us
    unnamed x13 -> x1, local copies, waits for them, and re-layouts: 4.15 us -> 1.57 us
    pallas_call x1, Pallas kernels: 45.6 us -> 44.6 us  [plane_body(): pl.pallas_call(functools.partial(plane_kernel, temper / math.sqrt(depth))...]
where the time goes in v3:
time: 46.4 us; the launch traced here: 46.2 us
  Pallas kernels  44.6 us (96%)
  local copies, waits for them, and re-layouts  1.57 us (3%)
    pallas_call x1, Pallas kernels, plane_body(): pl.pallas_call(functools.partial(plane_kernel, temper / math.sqrt(depth))...  44.6 us
    unnamed x1, local copies, waits for them, and re-layouts  1.57 us

profile of v3, /device:TPU:0, one launch (start us, length us, event | category | flops | bytes accessed | tf_op | source)
XLA Modules:
  0.0 46.2 jit_solution(5354724198275493007)
XLA Ops:
  0.0 44.6 %shard_map.64 = bf16[256,250]{1,0:T(8,128)(2,1)} custom-call(bf16[256,256]{1,0:T(8,128)(2,1)} %queries_ref.1, s32[1,256]{1,0:T(1,128)} %bitcast.4, s32[8,7]{1,0:T(8,128)} %mask_ref.1, bf16[128,1024]{1,0:T(8,128)(2,1)} %keys_ref.1, bf16[1000,128]{1,0:T(8,128)(2,1)} %bitcast.3, bf16[1,128]{1,0:T(2,128)(2,1)} %bitcast.5), custom_call_target="tpu_custom_call" | custom-call | tf_op jit(solution)/shard_map/pallas_call | solution.py:342
  44.7 1.6 %copy.8 = bf16[256,250]{1,0:T(8,128)(2,1)} copy(bf16[256,250]{1,0:T(8,128)(2,1)} %shard_map.64) | data formatting | bytes 256000

commit v4 on v3

--- a/solution.py
+++ b/solution.py
@@ -41,7 +41,6 @@
     bias,
     weights,
     stats_own,
-    numer_own,
     numer_out,
     numer_in,
     stats_in,
@@ -61,7 +60,7 @@
     half = queries_ref.shape[0] // 2
     rows = keys_ref.shape[0]
     part = labels_ref.shape[0] // 4
-    padded = lbuf.shape[2] // 2
+    padded = lbuf.shape[3]
     z, y = lax.div(cluster, 2), lax.rem(cluster, 2)
     x, core = lax.div(feat, 2), lax.rem(feat, 2)
     twin = (cluster, feat + 1 - 2 * core)
@@ -170,12 +169,23 @@
     lbuf[0] = jnp.zeros(lbuf.shape[1:], lbuf.dtype)
     loads[2].wait()
     for quarter in range(4):
-        start = (quarter % 2) * padded
-        lbuf[0, quarter // 2, start : start + part, :] = labels_buf[
+        lbuf[0, quarter // 2, quarter % 2, :part, :] = labels_buf[
             quarter * part : (quarter + 1) * part, :
         ]
-    labels_beside = [send(lbuf.at[0, side], lbuf.at[2, side], beside) for side in (1 - x, x)]
-    labels_twin = [send(lbuf.at[0, side], lbuf.at[1, side], twin) for side in (1 - x, x)]
+    quarters = [(1 - x, 0), (1 - x, 1), (x, 0), (x, 1)]
+    labels_beside, labels_twin, labels_relay = [], [], []
+    for side, turn in quarters:
+        labels_beside.append(send(lbuf.at[0, side, turn], lbuf.at[2, side, turn], beside))
+        labels_twin.append(send(lbuf.at[0, side, turn], lbuf.at[1, side, turn], twin))
+
+    def relay_labels(index):
+        side, turn = quarters[index]
+        labels_beside[index].wait_recv()
+        labels_relay.append(send(lbuf.at[2, side, turn], lbuf.at[3, side, turn], twin))
+
+    def labels_here(index):
+        labels_twin[index].wait_recv()
+        labels_relay[index].wait_recv()
 
     loads[3].wait()
     loads[4].wait()
@@ -236,16 +246,51 @@
         stats_own[step, 1:2, :] = total
         stats_own[step, 2:8, :] = jnp.zeros((6, half), jnp.float32)
 
-    def class_sum(step, side):
-        blocks = jnp.concatenate([lbuf[index, side] for index in range(4)], axis=1)
+    def class_sum(step, side, turn):
+        blocks = jnp.concatenate([lbuf[index, side, turn] for index in range(4)], axis=1)
         return jnp.dot(blocks, weights[step], preferred_element_type=jnp.float32)
 
-    numer_across, stats_across = {}, {}
-
-    def send_across(step):
-        numer_out[step] = class_sum(step, 1 - x).astype(jnp.bfloat16)
-        stats_across[step] = send(stats_own.at[step], stats_in.at[step], across)
-        numer_across[step] = send(numer_out.at[step], numer_in.at[step], across)
+    numer_across, stats_across, carried = {}, {}, {}
+
+    def send_across(step, turn):
+        numer_out[step, turn] = class_sum(step, 1 - x, turn).astype(jnp.bfloat16)
+        if turn == 0:
+            stats_across[step] = send(stats_own.at[step], stats_in.at[step], across)
+        numer_across[step, turn] = send(
+            numer_out.at[step, turn], numer_in.at[step, turn], across
+        )
+
+    place = 2 * z + core
+
+    def merge(step, turn):
+        numer = class_sum(step, x, turn)
+        floor = homes[step]
+        if turn == 0:
+            stats_across[step].wait_recv()
+            top_own, top_in = stats_own[step, 0:1, :], stats_in[step, 0:1, :]
+            top = jnp.maximum(top_own, top_in)
+            carry_own, carry_in = jnp.exp(top_own - top), jnp.exp(top_in - top)
+            total = stats_own[step, 1:2, :] * carry_own + stats_in[step, 1:2, :] * carry_in
+            carried[step] = carry_own, carry_in
+            home_stats_out[step, 0:1, :] = top
+            home_stats_out[step, 1:2, :] = total
+            home_stats_out[step, 2:8, :] = jnp.zeros((6, half), jnp.float32)
+            if step > 0:
+                for peer in (floor_peer(floor), mate(floor_peer(floor))):
+                    send(home_stats_out.at[step], home_stats_in.at[place], peer, (STATS, place))
+            else:
+                home_stats_in[place] = home_stats_out[0]
+                send(home_stats_out.at[0], home_stats_in.at[place], twin, (STATS, place))
+        carry_own, carry_in = carried[step]
+        numer_across[step, turn].wait_recv()
+        merged = numer * carry_own + numer_in[step, turn].astype(jnp.float32) * carry_in
+        home_out[step, turn] = merged.astype(jnp.bfloat16)
+        if step > 0:
+            peer = (2 * floor + y, 2 * x + turn)
+            send(home_out.at[step, turn], home_in.at[place], peer, (NUMER, place))
+        elif turn == 1:
+            home_in[place] = home_out[0, core]
+            send(home_out.at[0, 1 - core], home_in.at[place], twin, (NUMER, place))
 
     arrived(qbuf.at[z, 1 - x, 0], FIRST, z)
     arrived(qbuf.at[z, 1 - x, 1], SECOND, z)
@@ -263,47 +308,33 @@
     for index in range(4):
         bias[block(index), :] = spread(pbuf[index, 0:1, :], half)
     score(0)
+    score(1)
+    relay_labels(0)
+    score(2)
     relay(3)
-    score(1)
-    labels_beside[0].wait_recv()
-    labels_relay = [send(lbuf.at[2, 1 - x], lbuf.at[3, 1 - x], twin)]
-    score(2)
-    labels_twin[0].wait_recv()
-    labels_relay[0].wait_recv()
-    send_across(1)
-    send_across(2)
-    labels_beside[1].wait_recv()
-    labels_relay.append(send(lbuf.at[2, x], lbuf.at[3, x], twin))
+    labels_here(0)
+    send_across(2, 0)
+    relay_labels(1)
     score(3)
-    send_across(3)
-    send_across(0)
-    labels_twin[1].wait_recv()
-    labels_relay[1].wait_recv()
-
-    for step in (1, 2, 3, 0):
-        numer_own[step] = class_sum(step, x)
-        stats_across[step].wait_recv()
-        numer_across[step].wait_recv()
-        top_own, top_in = stats_own[step, 0:1, :], stats_in[step, 0:1, :]
-        top = jnp.maximum(top_own, top_in)
-        carry_own, carry_in = jnp.exp(top_own - top), jnp.exp(top_in - top)
-        total = stats_own[step, 1:2, :] * carry_own + stats_in[step, 1:2, :] * carry_in
-        merged = numer_own[step] * carry_own + numer_in[step].astype(jnp.float32) * carry_in
-        home_stats_out[step, 0:1, :] = top
-        home_stats_out[step, 1:2, :] = total
-        home_stats_out[step, 2:8, :] = jnp.zeros((6, half), jnp.float32)
-        home_out[step, 0] = merged[:padded].astype(jnp.bfloat16)
-        home_out[step, 1] = merged[padded:].astype(jnp.bfloat16)
-        place = 2 * z + core
-        peer = floor_peer(homes[step])
-        if step > 0:
-            send(home_stats_out.at[step], home_stats_in.at[place], peer, (STATS, place))
-            send(home_out.at[step, core], home_in.at[place], peer, (NUMER, place))
-        else:
-            home_stats_in[place] = home_stats_out[0]
-            home_in[place] = home_out[0, core]
-        send(home_stats_out.at[step], home_stats_in.at[place], mate(peer), (STATS, place))
-        send(home_out.at[step, 1 - core], home_in.at[place], mate(peer), (NUMER, place))
+    labels_here(1)
+    send_across(2, 1)
+    send_across(3, 0)
+    send_across(3, 1)
+    relay_labels(2)
+    send_across(1, 0)
+    send_across(1, 1)
+    labels_here(2)
+    merge(2, 0)
+    relay_labels(3)
+    labels_here(3)
+    merge(2, 1)
+    merge(3, 0)
+    send_across(0, 0)
+    send_across(0, 1)
+    merge(3, 1)
+    for step in (1, 0):
+        merge(step, 0)
+        merge(step, 1)
 
     for side in (0, 1):
         source = core if side == 0 else 1 - core
@@ -338,7 +369,7 @@
     padded = -(-part // 128) * 128
     vmem = pl.BlockSpec(memory_space=pltpu.VMEM)
     bf16, f32 = jnp.bfloat16, jnp.float32
-    copies = 80
+    copies = 96
     return pl.pallas_call(
         functools.partial(plane_kernel, temper / math.sqrt(depth)),
         out_shape=jax.ShapeDtypeStruct((2 * half, part), bf16),
@@ -352,14 +383,13 @@
             pltpu.VMEM((floors, 2, 2, half, width), bf16),
             pltpu.VMEM((floors, clusters, half), f32),
             pltpu.VMEM((4 * rows, depth), bf16),
-            pltpu.VMEM((4, 2, 2 * padded, rows), bf16),
+            pltpu.VMEM((4, 2, 2, padded, rows), bf16),
             pltpu.VMEM((4, 8, rows), f32),
             pltpu.VMEM((4 * rows, half), f32),
             pltpu.VMEM((floors, 4 * rows, half), bf16),
             pltpu.VMEM((floors, 8, half), f32),
-            pltpu.VMEM((floors, 2 * padded, half), f32),
-            pltpu.VMEM((floors, 2 * padded, half), bf16),
-            pltpu.VMEM((floors, 2 * padded, half), bf16),
+            pltpu.VMEM((floors, 2, padded, half), bf16),
+            pltpu.VMEM((floors, 2, padded, half), bf16),
             pltpu.VMEM((floors, 8, half), f32),
             pltpu.VMEM((floors, 2, padded, half), bf16),
             pltpu.VMEM((floors, 8, half), f32),

time: 46.4 us -> 43.5 us (0.938)
  Pallas kernels: 44.6 us -> 41.6 us
    pallas_call x1, Pallas kernels: 44.6 us -> 41.6 us  [plane_body(): pl.pallas_call(functools.partial(plane_kernel, temper / math.sqrt(depth))...]
where the time goes in v4:
time: 43.5 us; the launch traced here: 43.2 us
  Pallas kernels  41.6 us (96%)
  local copies, waits for them, and re-layouts  1.57 us (4%)
    pallas_call x1, Pallas kernels, plane_body(): pl.pallas_call(functools.partial(plane_kernel, temper / math.sqrt(depth))...  41.6 us
    unnamed x1, local copies, waits for them, and re-layouts  1.57 us

profile of v4, /device:TPU:0, one launch (start us, length us, event | category | flops | bytes accessed | tf_op | source)
XLA Modules:
  0.0 43.2 jit_solution(5775025985376709434)
XLA Ops:
  0.0 41.6 %shard_map.64 = bf16[256,250]{1,0:T(8,128)(2,1)} custom-call(bf16[256,256]{1,0:T(8,128)(2,1)} %queries_ref.1, s32[1,256]{1,0:T(1,128)} %bitcast.4, s32[8,7]{1,0:T(8,128)} %mask_ref.1, bf16[128,1024]{1,0:T(8,128)(2,1)} %keys_ref.1, bf16[1000,128]{1,0:T(8,128)(2,1)} %bitcast.3, bf16[1,128]{1,0:T(2,128)(2,1)} %bitcast.5), custom_call_target="tpu_custom_call" | custom-call | tf_op jit(solution)/shard_map/pallas_call | solution.py:373
  41.6 1.6 %copy.8 = bf16[256,250]{1,0:T(8,128)(2,1)} copy(bf16[256,250]{1,0:T(8,128)(2,1)} %shard_map.64) | data formatting | bytes 256000

commit v5 on v4

--- a/solution.py
+++ b/solution.py
@@ -130,15 +130,19 @@
             pl.when(only)(copy.start)
         return copy
 
-    def arrived(ref, kind, index):
-        pltpu.make_async_remote_copy(
+    def arrived(ref, kind, index, only=None):
+        copy = pltpu.make_async_remote_copy(
             src_ref=ref,
             dst_ref=ref,
             send_sem=send_sem.at[0],
             recv_sem=home_sem.at[kind, index],
             device_id=twin,
             device_id_type=MESH,
-        ).wait_recv()
+        )
+        if only is None:
+            copy.wait_recv()
+        else:
+            pl.when(only)(copy.wait_recv)
 
     mine = pl.ds(pl.multiple_of(core * half, half), half)
     other = pl.ds(pl.multiple_of((1 - core) * half, half), half)
@@ -162,9 +166,9 @@
     prior_beside = send(pbuf.at[0], pbuf.at[2], beside)
     prior_twin = send(pbuf.at[0], pbuf.at[1], twin)
 
-    def pass_on(home, kind, ref, start=False):
-        send(ref, ref, above, (kind, home), (home <= z if start else home < z) & up)
-        send(ref, ref, below, (kind, home), (home >= z if start else home > z) & down)
+    def pass_on(home, kind, ref, only):
+        send(ref, ref, above, (kind, home), only & (home <= z) & up)
+        send(ref, ref, below, (kind, home), only & (home >= z) & down)
 
     lbuf[0] = jnp.zeros(lbuf.shape[1:], lbuf.dtype)
     loads[2].wait()
@@ -205,16 +209,16 @@
     for home in homes[1:]:
         send(vbuf.at[z], vbuf.at[z], floor_peer(home), (SEEN, z))
 
-    def relay(step):
+    def relay(step, only):
         home = homes[step]
         first, second, extra = qbuf.at[home, x, 0], qbuf.at[home, x, 1], qbuf.at[home, 1 - x, 1]
-        arrived(first, FIRST, home)
-        pass_on(home, FIRST, first)
-        send(first, first, across, (ACROSS, home))
-        arrived(second, SECOND, home)
-        pass_on(home, SECOND, second)
-        arrived(extra, EXTRA, home)
-        pass_on(home, EXTRA, extra)
+        arrived(first, FIRST, home, only)
+        pass_on(home, FIRST, first, only)
+        send(first, first, across, (ACROSS, home), only)
+        arrived(second, SECOND, home, only)
+        pass_on(home, SECOND, second, only)
+        arrived(extra, EXTRA, home, only)
+        pass_on(home, EXTRA, extra, only)
 
     def score(step):
         home = homes[step]
@@ -292,15 +296,16 @@
             home_in[place] = home_out[0, core]
             send(home_out.at[0, 1 - core], home_in.at[place], twin, (NUMER, place))
 
+    always, inside = z >= 0, inner > 0
     arrived(qbuf.at[z, 1 - x, 0], FIRST, z)
     arrived(qbuf.at[z, 1 - x, 1], SECOND, z)
-    pass_on(z, EXTRA, qbuf.at[z, 1 - x, 1], True)
-    relay(1)
+    pass_on(z, EXTRA, qbuf.at[z, 1 - x, 1], always)
+    relay(1, always)
+    relay(2, always)
     keys_beside.wait_recv()
     prior_beside.wait_recv()
     keys_relay = send(kbuf.at[block(2)], kbuf.at[block(3)], twin)
     prior_relay = send(pbuf.at[2], pbuf.at[3], twin)
-    relay(2)
     for copy in (keys_twin, prior_twin, keys_relay, prior_relay, query_twin):
         copy.wait_recv()
     loads[0].wait()
@@ -308,16 +313,17 @@
     for index in range(4):
         bias[block(index), :] = spread(pbuf[index, 0:1, :], half)
     score(0)
+    relay(3, inside)
     score(1)
     relay_labels(0)
     score(2)
-    relay(3)
     labels_here(0)
     send_across(2, 0)
     relay_labels(1)
-    score(3)
+    relay(3, inner == 0)
     labels_here(1)
     send_across(2, 1)
+    score(3)
     send_across(3, 0)
     send_across(3, 1)
     relay_labels(2)
@@ -369,7 +375,7 @@
     padded = -(-part // 128) * 128
     vmem = pl.BlockSpec(memory_space=pltpu.VMEM)
     bf16, f32 = jnp.bfloat16, jnp.float32
-    copies = 96
+    copies = 112
     return pl.pallas_call(
         functools.partial(plane_kernel, temper / math.sqrt(depth)),
         out_shape=jax.ShapeDtypeStruct((2 * half, part), bf16),

time: 43.5 us -> 46.8 us (1.076)
  Pallas kernels: 41.6 us -> 45 us
    pallas_call x1, Pallas kernels: 41.6 us -> 45 us  [plane_body(): pl.pallas_call(functools.partial(plane_kernel, temper / math.sqrt(depth))...]
where the time goes in v5:
time: 46.8 us; the launch traced here: 46.5 us
  Pallas kernels  45 us (96%)
  local copies, waits for them, and re-layouts  1.57 us (3%)
    pallas_call x1, Pallas kernels, plane_body(): pl.pallas_call(functools.partial(plane_kernel, temper / math.sqrt(depth))...  45 us
    unnamed x1, local copies, waits for them, and re-layouts  1.57 us

profile of v5, /device:TPU:0, one launch (start us, length us, event | category | flops | bytes accessed | tf_op | source)
XLA Modules:
  0.0 46.5 jit_solution(12340800325719515891)
XLA Ops:
  0.0 45.0 %shard_map.64 = bf16[256,250]{1,0:T(8,128)(2,1)} custom-call(bf16[256,256]{1,0:T(8,128)(2,1)} %queries_ref.1, s32[1,256]{1,0:T(1,128)} %bitcast.4, s32[8,7]{1,0:T(8,128)} %mask_ref.1, bf16[128,1024]{1,0:T(8,128)(2,1)} %keys_ref.1, bf16[1000,128]{1,0:T(8,128)(2,1)} %bitcast.3, bf16[1,128]{1,0:T(2,128)(2,1)} %bitcast.5), custom_call_target="tpu_custom_call" | custom-call | tf_op jit(solution)/shard_map/pallas_call | solution.py:379
  45.0 1.6 %copy.8 = bf16[256,250]{1,0:T(8,128)(2,1)} copy(bf16[256,250]{1,0:T(8,128)(2,1)} %shard_map.64) | data formatting | bytes 256000

commit v6 on v5

--- a/solution.py
+++ b/solution.py
@@ -71,7 +71,7 @@
         return (peer[0], peer[1] + 1 - 2 * core)
 
     above, below = (cluster + 2, feat), (cluster - 2, feat)
-    FIRST, SECOND, EXTRA, ACROSS, SEEN, NUMER, STATS = range(7)
+    FIRST, SECOND, ACROSS, ACROSS_SECOND, SEEN, NUMER, STATS = range(7)
 
     loads = [
         pltpu.make_async_copy(src, dst, load_sem.at[index])
@@ -211,19 +211,17 @@
 
     def relay(step, only):
         home = homes[step]
-        first, second, extra = qbuf.at[home, x, 0], qbuf.at[home, x, 1], qbuf.at[home, 1 - x, 1]
-        arrived(first, FIRST, home, only)
-        pass_on(home, FIRST, first, only)
-        send(first, first, across, (ACROSS, home), only)
-        arrived(second, SECOND, home, only)
-        pass_on(home, SECOND, second, only)
-        arrived(extra, EXTRA, home, only)
-        pass_on(home, EXTRA, extra, only)
+        for turn, (kind, copied) in enumerate(((FIRST, ACROSS), (SECOND, ACROSS_SECOND))):
+            part_here = qbuf.at[home, x, turn]
+            arrived(part_here, kind, home, only)
+            pass_on(home, kind, part_here, only)
+            send(part_here, part_here, across, (copied, home), only)
 
     def score(step):
         home = homes[step]
         if step > 0:
             arrived(qbuf.at[home, 1 - x, 0], ACROSS, home)
+            arrived(qbuf.at[home, 1 - x, 1], ACROSS_SECOND, home)
             arrived(vbuf.at[home], SEEN, home)
         width = qbuf.shape[4]
         scores = jnp.zeros((4 * rows, half), jnp.float32)
@@ -296,16 +294,17 @@
             home_in[place] = home_out[0, core]
             send(home_out.at[0, 1 - core], home_in.at[place], twin, (NUMER, place))
 
-    always, inside = z >= 0, inner > 0
-    arrived(qbuf.at[z, 1 - x, 0], FIRST, z)
-    arrived(qbuf.at[z, 1 - x, 1], SECOND, z)
-    pass_on(z, EXTRA, qbuf.at[z, 1 - x, 1], always)
+    always, inside, at_end = z >= 0, inner > 0, inner == 0
     relay(1, always)
-    relay(2, always)
+    relay(2, inside)
     keys_beside.wait_recv()
     prior_beside.wait_recv()
     keys_relay = send(kbuf.at[block(2)], kbuf.at[block(3)], twin)
     prior_relay = send(pbuf.at[2], pbuf.at[3], twin)
+    relay(3, inside)
+    relay(2, at_end)
+    arrived(qbuf.at[z, 1 - x, 0], FIRST, z)
+    arrived(qbuf.at[z, 1 - x, 1], SECOND, z)
     for copy in (keys_twin, prior_twin, keys_relay, prior_relay, query_twin):
         copy.wait_recv()
     loads[0].wait()
@@ -313,14 +312,13 @@
     for index in range(4):
         bias[block(index), :] = spread(pbuf[index, 0:1, :], half)
     score(0)
-    relay(3, inside)
     score(1)
     relay_labels(0)
     score(2)
     labels_here(0)
     send_across(2, 0)
     relay_labels(1)
-    relay(3, inner == 0)
+    relay(3, at_end)
     labels_here(1)
     send_across(2, 1)
     score(3)

time: 46.8 us -> 43.2 us (0.923)
  Pallas kernels: 45 us -> 41.5 us
    pallas_call x1, Pallas kernels: 45 us -> 41.5 us  [plane_body(): pl.pallas_call(functools.partial(plane_kernel, temper / math.sqrt(depth))...]
where the time goes in v6:
time: 43.2 us; the launch traced here: 43.1 us
  Pallas kernels  41.5 us (96%)
  local copies, waits for them, and re-layouts  1.57 us (4%)
    pallas_call x1, Pallas kernels, plane_body(): pl.pallas_call(functools.partial(plane_kernel, temper / math.sqrt(depth))...  41.5 us
    unnamed x1, local copies, waits for them, and re-layouts  1.57 us

profile of v6, /device:TPU:0, one launch (start us, length us, event | category | flops | bytes accessed | tf_op | source)
XLA Modules:
  0.0 43.1 jit_solution(10912622902339594242)
XLA Ops:
  0.0 41.5 %shard_map.64 = bf16[256,250]{1,0:T(8,128)(2,1)} custom-call(bf16[256,256]{1,0:T(8,128)(2,1)} %queries_ref.1, s32[1,256]{1,0:T(1,128)} %bitcast.4, s32[8,7]{1,0:T(8,128)} %mask_ref.1, bf16[128,1024]{1,0:T(8,128)(2,1)} %keys_ref.1, bf16[1000,128]{1,0:T(8,128)(2,1)} %bitcast.3, bf16[1,128]{1,0:T(2,128)(2,1)} %bitcast.5), custom_call_target="tpu_custom_call" | custom-call | tf_op jit(solution)/shard_map/pallas_call | solution.py:377
  41.5 1.6 %copy.8 = bf16[256,250]{1,0:T(8,128)(2,1)} copy(bf16[256,250]{1,0:T(8,128)(2,1)} %shard_map.64) | data formatting | bytes 256000

commit v7 on v6

--- a/solution.py
+++ b/solution.py
@@ -223,16 +223,12 @@
             arrived(qbuf.at[home, 1 - x, 0], ACROSS, home)
             arrived(qbuf.at[home, 1 - x, 1], ACROSS_SECOND, home)
             arrived(vbuf.at[home], SEEN, home)
-        width = qbuf.shape[4]
-        scores = jnp.zeros((4 * rows, half), jnp.float32)
-        for quarter in range(4):
-            scores = scores + lax.dot_general(
-                kbuf[:, quarter * width : (quarter + 1) * width],
-                qbuf[home, quarter // 2, quarter % 2],
-                (((1,), (1,)), ((), ())),
-                preferred_element_type=jnp.float32,
-            )
-        scores = scores * scale
+        features = jnp.concatenate(
+            [qbuf[home, quarter // 2, quarter % 2] for quarter in range(4)], axis=1
+        )
+        scores = scale * lax.dot_general(
+            kbuf[...], features, (((1,), (1,)), ((), ())), preferred_element_type=jnp.float32
+        )
         near = vbuf[home, pl.ds(cluster, 1), :]
         far = vbuf[home, pl.ds(cluster + 1 - 2 * y, 1), :]
         pieces = []
@@ -311,7 +307,6 @@
     loads[5].wait()
     for index in range(4):
         bias[block(index), :] = spread(pbuf[index, 0:1, :], half)
-    score(0)
     score(1)
     relay_labels(0)
     score(2)
@@ -324,6 +319,7 @@
     score(3)
     send_across(3, 0)
     send_across(3, 1)
+    score(0)
     relay_labels(2)
     send_across(1, 0)
     send_across(1, 1)

time: 43.2 us -> 44.1 us (1.021)
  Pallas kernels: 41.5 us -> 42.4 us
    pallas_call x1, Pallas kernels: 41.5 us -> 42.4 us  [plane_body(): pl.pallas_call(functools.partial(plane_kernel, temper / math.sqrt(depth))...]
where the time goes in v7:
time: 44.1 us; the launch traced here: 43.9 us
  Pallas kernels  42.4 us (96%)
  local copies, waits for them, and re-layouts  1.57 us (4%)
    pallas_call x1, Pallas kernels, plane_body(): pl.pallas_call(functools.partial(plane_kernel, temper / math.sqrt(depth))...  42.4 us
    unnamed x1, local copies, waits for them, and re-layouts  1.57 us

profile of v7, /device:TPU:0, one launch (start us, length us, event | category | flops | bytes accessed | tf_op | source)
XLA Modules:
  0.0 43.9 jit_solution(7141536665718769465)
XLA Ops:
  0.0 42.4 %shard_map.64 = bf16[256,250]{1,0:T(8,128)(2,1)} custom-call(bf16[256,256]{1,0:T(8,128)(2,1)} %queries_ref.1, s32[1,256]{1,0:T(1,128)} %bitcast.4, s32[8,7]{1,0:T(8,128)} %mask_ref.1, bf16[128,1024]{1,0:T(8,128)(2,1)} %keys_ref.1, bf16[1000,128]{1,0:T(8,128)(2,1)} %bitcast.3, bf16[1,128]{1,0:T(2,128)(2,1)} %bitcast.5), custom_call_target="tpu_custom_call" | custom-call | tf_op jit(solution)/shard_map/pallas_call | solution.py:373
  42.4 1.6 %copy.8 = bf16[256,250]{1,0:T(8,128)(2,1)} copy(bf16[256,250]{1,0:T(8,128)(2,1)} %shard_map.64) | data formatting | bytes 256000

commit v8 on v7

--- a/solution.py
+++ b/solution.py
@@ -71,7 +71,7 @@
         return (peer[0], peer[1] + 1 - 2 * core)
 
     above, below = (cluster + 2, feat), (cluster - 2, feat)
-    FIRST, SECOND, ACROSS, ACROSS_SECOND, SEEN, NUMER, STATS = range(7)
+    FIRST, SECOND, ACROSS, ACROSS_SECOND, EXTRA, SEEN, NUMER, STATS = range(8)
 
     loads = [
         pltpu.make_async_copy(src, dst, load_sem.at[index])
@@ -151,6 +151,7 @@
     def block(index):
         return pl.ds(index * rows, rows)
 
+    keys_beside = send(keys_ref, kbuf.at[block(2)], beside)
     own, piece = qbuf.at[z, x, core], core
     query_twin = send(queries_ref.at[other], own, twin)
     send(queries_ref.at[mine], own, above, (FIRST + piece, z), up)
@@ -159,7 +160,6 @@
     send(queries_ref.at[other], own, mate(below), (FIRST + piece, z), down)
     send(queries_ref.at[mine], own, across, (FIRST + piece, z))
     send(queries_ref.at[other], own, mate(across), (FIRST + piece, z))
-    keys_beside = send(keys_ref, kbuf.at[block(2)], beside)
     keys_twin = send(keys_ref, kbuf.at[block(1)], twin)
     loads[1].wait()
     pbuf[0] = jnp.broadcast_to(prior_buf[...].astype(jnp.float32), (8, rows))
@@ -209,19 +209,30 @@
     for home in homes[1:]:
         send(vbuf.at[z], vbuf.at[z], floor_peer(home), (SEEN, z))
 
+    early, late = pl.ds(0, half // 2), pl.ds(half // 2, half // 2)
+
     def relay(step, only):
         home = homes[step]
         for turn, (kind, copied) in enumerate(((FIRST, ACROSS), (SECOND, ACROSS_SECOND))):
             part_here = qbuf.at[home, x, turn]
             arrived(part_here, kind, home, only)
             pass_on(home, kind, part_here, only)
+            if turn == 1:
+                part_here = part_here.at[late]
             send(part_here, part_here, across, (copied, home), only)
+
+    def extra_piece(home):
+        return qbuf.at[home, 1 - x, 1, early]
+
+    def relay_extra(step, only):
+        arrived(extra_piece(homes[step]), EXTRA, homes[step], only)
+        pass_on(homes[step], EXTRA, extra_piece(homes[step]), only)
 
     def score(step):
         home = homes[step]
         if step > 0:
             arrived(qbuf.at[home, 1 - x, 0], ACROSS, home)
-            arrived(qbuf.at[home, 1 - x, 1], ACROSS_SECOND, home)
+            arrived(qbuf.at[home, 1 - x, 1, late], ACROSS_SECOND, home)
             arrived(vbuf.at[home], SEEN, home)
         features = jnp.concatenate(
             [qbuf[home, quarter // 2, quarter % 2] for quarter in range(4)], axis=1
@@ -292,34 +303,40 @@
 
     always, inside, at_end = z >= 0, inner > 0, inner == 0
     relay(1, always)
+    arrived(qbuf.at[z, 1 - x, 0], FIRST, z)
+    arrived(qbuf.at[z, 1 - x, 1], SECOND, z)
+    pass_on(z, EXTRA, extra_piece(z), always)
     relay(2, inside)
     keys_beside.wait_recv()
     prior_beside.wait_recv()
     keys_relay = send(kbuf.at[block(2)], kbuf.at[block(3)], twin)
     prior_relay = send(pbuf.at[2], pbuf.at[3], twin)
+    relay_extra(1, always)
+    relay_extra(2, inside)
     relay(3, inside)
+    relay_extra(3, inside)
     relay(2, at_end)
-    arrived(qbuf.at[z, 1 - x, 0], FIRST, z)
-    arrived(qbuf.at[z, 1 - x, 1], SECOND, z)
     for copy in (keys_twin, prior_twin, keys_relay, prior_relay, query_twin):
         copy.wait_recv()
     loads[0].wait()
     loads[5].wait()
     for index in range(4):
         bias[block(index), :] = spread(pbuf[index, 0:1, :], half)
+    score(0)
     score(1)
     relay_labels(0)
+    relay_extra(2, at_end)
     score(2)
     labels_here(0)
     send_across(2, 0)
     relay_labels(1)
     relay(3, at_end)
+    relay_extra(3, at_end)
     labels_here(1)
     send_across(2, 1)
     score(3)
     send_across(3, 0)
     send_across(3, 1)
-    score(0)
     relay_labels(2)
     send_across(1, 0)
     send_across(1, 1)
@@ -397,7 +414,7 @@
             pltpu.VMEM((2 * floors, 8, half), f32),
             pltpu.SemaphoreType.DMA((copies,)),
             pltpu.SemaphoreType.DMA((copies,)),
-            pltpu.SemaphoreType.DMA((7, 2 * floors)),
+            pltpu.SemaphoreType.DMA((8, 2 * floors)),
             pltpu.SemaphoreType.DMA((6,)),
         ],
         compiler_params=pltpu.CompilerParams(

time: 44.1 us -> 42.5 us (0.964)
  Pallas kernels: 42.4 us -> 40.8 us
    pallas_call x1, Pallas kernels: 42.4 us -> 40.8 us  [plane_body(): pl.pallas_call(functools.partial(plane_kernel, temper / math.sqrt(depth))...]
where the time goes in v8:
time: 42.5 us; the launch traced here: 42.3 us
  Pallas kernels  40.8 us (96%)
  local copies, waits for them, and re-layouts  1.57 us (4%)
    pallas_call x1, Pallas kernels, plane_body(): pl.pallas_call(functools.partial(plane_kernel, temper / math.sqrt(depth))...  40.8 us
    unnamed x1, local copies, waits for them, and re-layouts  1.57 us

profile of v8, /device:TPU:0, one launch (start us, length us, event | category | flops | bytes accessed | tf_op | source)
XLA Modules:
  0.0 42.3 jit_solution(10794626111186913144)
XLA Ops:
  0.0 40.8 %shard_map.64 = bf16[256,250]{1,0:T(8,128)(2,1)} custom-call(bf16[256,256]{1,0:T(8,128)(2,1)} %queries_ref.1, s32[1,256]{1,0:T(1,128)} %bitcast.4, s32[8,7]{1,0:T(8,128)} %mask_ref.1, bf16[128,1024]{1,0:T(8,128)(2,1)} %keys_ref.1, bf16[1000,128]{1,0:T(8,128)(2,1)} %bitcast.3, bf16[1,128]{1,0:T(2,128)(2,1)} %bitcast.5), custom_call_target="tpu_custom_call" | custom-call | tf_op jit(solution)/shard_map/pallas_call | solution.py:390
  40.8 1.6 %copy.8 = bf16[256,250]{1,0:T(8,128)(2,1)} copy(bf16[256,250]{1,0:T(8,128)(2,1)} %shard_map.64) | data formatting | bytes 256000

commit v9 on v8

--- a/solution.py
+++ b/solution.py
@@ -330,10 +330,10 @@
     labels_here(0)
     send_across(2, 0)
     relay_labels(1)
+    labels_here(1)
+    send_across(2, 1)
     relay(3, at_end)
     relay_extra(3, at_end)
-    labels_here(1)
-    send_across(2, 1)
     score(3)
     send_across(3, 0)
     send_across(3, 1)

time: 42.5 us -> 44.6 us (1.049)
  Pallas kernels: 40.8 us -> 42.7 us
    pallas_call x1, Pallas kernels: 40.8 us -> 42.7 us  [plane_body(): pl.pallas_call(functools.partial(plane_kernel, temper / math.sqrt(depth))...]
where the time goes in v9:
time: 44.6 us; the launch traced here: 44.3 us
  Pallas kernels  42.7 us (96%)
  local copies, waits for them, and re-layouts  1.57 us (4%)
    pallas_call x1, Pallas kernels, plane_body(): pl.pallas_call(functools.partial(plane_kernel, temper / math.sqrt(depth))...  42.7 us
    unnamed x1, local copies, waits for them, and re-layouts  1.57 us

profile of v9, /device:TPU:0, one launch (start us, length us, event | category | flops | bytes accessed | tf_op | source)
XLA Modules:
  0.0 44.3 jit_solution(13445386978492420449)
XLA Ops:
  0.0 42.7 %shard_map.64 = bf16[256,250]{1,0:T(8,128)(2,1)} custom-call(bf16[256,256]{1,0:T(8,128)(2,1)} %queries_ref.1, s32[1,256]{1,0:T(1,128)} %bitcast.4, s32[8,7]{1,0:T(8,128)} %mask_ref.1, bf16[128,1024]{1,0:T(8,128)(2,1)} %keys_ref.1, bf16[1000,128]{1,0:T(8,128)(2,1)} %bitcast.3, bf16[1,128]{1,0:T(2,128)(2,1)} %bitcast.5), custom_call_target="tpu_custom_call" | custom-call | tf_op jit(solution)/shard_map/pallas_call | solution.py:390
  42.7 1.6 %copy.8 = bf16[256,250]{1,0:T(8,128)(2,1)} copy(bf16[256,250]{1,0:T(8,128)(2,1)} %shard_map.64) | data formatting | bytes 256000
